TPU v7x, 32 devices: a whole 2x2x4 slice. The times are simulated.
32 devices in a mesh: tensor: 4 (over x, core), frames: 8 (over z, y).
Axes of the slice: x: 2, y: 2, z: 4, core: 2. Of those that a mesh axis runs over, the one named last changes fastest.
Arguments:
- tokens: bfloat16 [8, 8, 256, 1024], P('frames', None, 'tensor'), may hold values from -6 to 6
- codes: int32 [8, 8], P('frames'), may hold values from 0 to 7
- table: bfloat16 [8, 1024], replicated, may hold values from -6 to 6
- gain_space: bfloat16 [1024], replicated, may hold values from 0.5 to 1.5
- gain_time: bfloat16 [1024], replicated, may hold values from 0.5 to 1.5
- gain_ffn: bfloat16 [1024], replicated, may hold values from 0.5 to 1.5
- w_qkv_space: bfloat16 [1024, 3, 1024], P(None, None, 'tensor'), may hold values from -0.1875 to 0.1875
- w_out_space: bfloat16 [1024, 1024], P('tensor'), may hold values from -1.5 to 1.5
- w_qkv_time: bfloat16 [1024, 3, 1024], P(None, None, 'tensor'), may hold values from -0.1875 to 0.1875
- w_out_time: bfloat16 [1024, 1024], P('tensor'), may hold values from -0.75 to 0.75
- w_up: bfloat16 [1024, 4096], P(None, 'tensor'), may hold values from -0.1875 to 0.1875
- w_down: bfloat16 [4096, 1024], P('tensor'), may hold values from -0.09375 to 0.09375
- cotangent: bfloat16 [8, 8, 256, 1024], P('frames', None, 'tensor'), may hold values from -6 to 6
Outputs:
- mixed: bfloat16 [8, 8, 256, 1024], P('frames', None, 'tensor')
- grad_tokens: float32 [8, 8, 256, 1024], P('frames', None, 'tensor')
- grad_table: float32 [8, 1024], replicated
- grad_gain_space: float32 [1024], replicated
- grad_gain_time: float32 [1024], replicated
- grad_gain_ffn: float32 [1024], replicated
- grad_qkv_space: float32 [1024, 3, 1024], P(None, None, 'tensor')
- grad_out_space: float32 [1024, 1024], P('tensor')
- grad_qkv_time: float32 [1024, 3, 1024], P(None, None, 'tensor')
- grad_out_time: float32 [1024, 1024], P('tensor')
- grad_up: float32 [1024, 4096], P(None, 'tensor')
- grad_down: float32 [4096, 1024], P('tensor')
All inputs are finite; a program needn't handle non-finite values.
Results may differ from a plain program's by a relative error of at most 0.019.
Values may be sent and summed in bfloat16 or wider, within the bound.
A program may use at most 576 MiB of HBM per device.

v0:
```python
import jax
import jax.numpy as jnp
from jax import lax
from jax.sharding import PartitionSpec as P

HD = 64


EPS = 1e-06


def norm_rows(values, gain_vec):
    factor = lax.rsqrt(jnp.mean(values * values, axis=-1, keepdims=True) + EPS)
    return values * factor * gain_vec


def spread(values):
    return lax.all_gather(values, "tensor", axis=2, tiled=True)


def collect(values):
    return lax.psum_scatter(values, "tensor", scatter_dimension=2, tiled=True)


def spread_back(values):
    return lax.all_gather(values, "tensor", axis=2, tiled=True)


def collect_back(values):
    return lax.psum_scatter(
        values.astype(jnp.bfloat16), "tensor", scatter_dimension=2, tiled=True
    ).astype(jnp.float32)


def split_heads(values):
    return values.reshape(values.shape[:-1] + (values.shape[-1] // HD, HD))


def merge_heads(values):
    return values.reshape(values.shape[:-2] + (values.shape[-2] * values.shape[-1],))


def log_total(scores):
    largest = jnp.max(scores, axis=-1, keepdims=True)
    return largest + jnp.log(jnp.sum(jnp.exp(scores - largest), axis=-1, keepdims=True))


def project(stream, gain_vec, w_qkv):
    normed = norm_rows(stream, gain_vec).astype(jnp.bfloat16)
    gathered = spread(normed)
    packed = jnp.einsum(
        "fcsd,dke->fcske", gathered, w_qkv, preferred_element_type=jnp.float32
    ).astype(jnp.bfloat16)
    return (gathered, packed[..., 0, :], packed[..., 1, :], packed[..., 2, :])


def space_scores(queries, keys_in):
    return jnp.einsum(
        "fcshe,fcthe->fchst",
        split_heads(queries),
        split_heads(keys_in),
        preferred_element_type=jnp.float32,
    ) * HD ** (-0.5)


def space_forward(queries, keys_in, values):
    scores = space_scores(queries, keys_in)
    log_norm = log_total(scores)
    soft_weights = jnp.exp(scores - log_norm).astype(jnp.bfloat16)
    result = jnp.einsum(
        "fchst,fcthe->fcshe", soft_weights, split_heads(values), preferred_element_type=jnp.float32
    )
    return (merge_heads(result).astype(jnp.bfloat16), log_norm)


def space_backward(queries, keys_in, values, log_norm, grad_out):
    scores = space_scores(queries, keys_in)
    soft_weights = jnp.exp(scores - log_norm)
    grad_heads = split_heads(grad_out)
    grad_soft = jnp.einsum(
        "fcshe,fcthe->fchst", grad_heads, split_heads(values), preferred_element_type=jnp.float32
    )
    row_dot = jnp.sum(grad_soft * soft_weights, axis=-1, keepdims=True)
    grad_scores = (soft_weights * (grad_soft - row_dot)).astype(jnp.bfloat16)
    grad_q = jnp.einsum(
        "fchst,fcthe->fcshe", grad_scores, split_heads(keys_in), preferred_element_type=jnp.float32
    ) * HD ** (-0.5)
    grad_k = jnp.einsum(
        "fchst,fcshe->fcthe", grad_scores, split_heads(queries), preferred_element_type=jnp.float32
    ) * HD ** (-0.5)
    grad_v = jnp.einsum(
        "fchst,fcshe->fcthe",
        soft_weights.astype(jnp.bfloat16),
        grad_heads,
        preferred_element_type=jnp.float32,
    )
    return (
        merge_heads(grad_q).astype(jnp.bfloat16),
        merge_heads(grad_k).astype(jnp.bfloat16),
        merge_heads(grad_v).astype(jnp.bfloat16),
    )


def time_scores(queries, keys_in, first_frame):
    scores = jnp.einsum(
        "fcphe,gcphe->cphfg",
        split_heads(queries),
        split_heads(keys_in),
        preferred_element_type=jnp.float32,
    ) * HD ** (-0.5)
    query_idx = first_frame + jnp.arange(queries.shape[0], dtype=jnp.int32)
    key_idx = jnp.arange(keys_in.shape[0], dtype=jnp.int32)
    return jnp.where(key_idx[None, :] <= query_idx[:, None], scores, -1e30)


def time_forward(queries, keys_in, values, first_frame):
    scores = time_scores(queries, keys_in, first_frame)
    log_norm = log_total(scores)
    soft_weights = jnp.exp(scores - log_norm).astype(jnp.bfloat16)
    result = jnp.einsum(
        "cphfg,gcphe->fcphe", soft_weights, split_heads(values), preferred_element_type=jnp.float32
    )
    return (merge_heads(result).astype(jnp.bfloat16), log_norm)


def time_probs(queries, keys_in, values, log_norm, grad_out, first_frame):
    scores = time_scores(queries, keys_in, first_frame)
    soft_weights = jnp.exp(scores - log_norm)
    grad_soft = jnp.einsum(
        "fcphe,gcphe->cphfg",
        split_heads(grad_out),
        split_heads(values),
        preferred_element_type=jnp.float32,
    )
    row_dot = jnp.sum(grad_soft * soft_weights, axis=-1, keepdims=True)
    grad_scores = (soft_weights * (grad_soft - row_dot)).astype(jnp.bfloat16)
    return (grad_scores, soft_weights.astype(jnp.bfloat16))


def time_query_grads(grad_scores, keys_in):
    result = jnp.einsum(
        "cphfg,gcphe->fcphe", grad_scores, split_heads(keys_in), preferred_element_type=jnp.float32
    )
    return (merge_heads(result) * HD ** (-0.5)).astype(jnp.bfloat16)


def time_key_grads(grad_scores, soft_weights, queries, grad_out):
    grad_k = jnp.einsum(
        "cphfg,fcphe->gcphe", grad_scores, split_heads(queries), preferred_element_type=jnp.float32
    ) * HD ** (-0.5)
    grad_v = jnp.einsum(
        "cphfg,fcphe->gcphe",
        soft_weights,
        split_heads(grad_out),
        preferred_element_type=jnp.float32,
    )
    return (merge_heads(grad_k), merge_heads(grad_v))


def out_backward(attended, w_out, grad_stream):
    grad_y = spread_back(grad_stream.astype(jnp.bfloat16))
    grad_w = jnp.einsum("fcse,fcsd->ed", attended, grad_y, preferred_element_type=jnp.float32)
    grad_in = jnp.einsum("fcsd,ed->fcse", grad_y, w_out, preferred_element_type=jnp.float32)
    return (grad_w, grad_in)


def norm_backward(partial_value, stream, gain_vec):
    grad_normed = collect_back(partial_value)
    _, pullback = jax.vjp(norm_rows, stream, gain_vec)
    return pullback(grad_normed)


def qkv_backward(gathered, w_qkv, grad_q, grad_k, grad_v, stream, gain_vec):
    packed = jnp.stack([grad_q, grad_k, grad_v], axis=-2)
    grad_w = jnp.einsum("fcsd,fcske->dke", gathered, packed, preferred_element_type=jnp.float32)
    partial_value = jnp.einsum("fcske,dke->fcsd", packed, w_qkv, preferred_element_type=jnp.float32)
    grad_stream, grad_gain = norm_backward(partial_value, stream, gain_vec)
    return (grad_w, grad_stream, grad_gain)


def body(
    tokens,
    codes,
    table,
    gain_space,
    gain_time,
    gain_ffn,
    w_qkv_space,
    w_out_space,
    w_qkv_time,
    w_out_time,
    w_up,
    w_down,
    cotangent,
):
    gain_sp = gain_space.astype(jnp.float32)
    gain_tm = gain_time.astype(jnp.float32)
    gain_ff = gain_ffn.astype(jnp.float32)
    one_hot = (codes[..., None] == jnp.arange(table.shape[0], dtype=jnp.int32)).astype(jnp.float32)
    added = jnp.sum(one_hot[..., None] * table.astype(jnp.float32), axis=-2)
    stream_zero = tokens.astype(jnp.float32) + added[:, :, None, :]
    gathered_sp, queries_sp, keys_sp, values_sp = project(stream_zero, gain_sp, w_qkv_space)
    attended_sp, log_norm_sp = space_forward(queries_sp, keys_sp, values_sp)
    stream_one = stream_zero + collect(
        jnp.einsum("fcse,ed->fcsd", attended_sp, w_out_space, preferred_element_type=jnp.float32)
    )
    gathered_tm, queries_tm, keys_tm, values_tm = project(stream_one, gain_tm, w_qkv_time)
    keys_every, values_every = (
        lax.all_gather(keys_tm, "frames", axis=0, tiled=True),
        lax.all_gather(values_tm, "frames", axis=0, tiled=True),
    )
    my_frame = lax.axis_index("frames")
    attended_tm, log_norm_tm = time_forward(queries_tm, keys_every, values_every, my_frame)
    stream_two = stream_one + collect(
        jnp.einsum("fcse,ed->fcsd", attended_tm, w_out_time, preferred_element_type=jnp.float32)
    )
    normed_ff = norm_rows(stream_two, gain_ff).astype(jnp.bfloat16)
    gathered_ff = spread(normed_ff)
    hidden_pre = jnp.einsum("fcsd,dh->fcsh", gathered_ff, w_up, preferred_element_type=jnp.float32)
    activated = jax.nn.gelu(hidden_pre).astype(jnp.bfloat16)
    stream_out = stream_two + collect(
        jnp.einsum("fcsh,hd->fcsd", activated, w_down, preferred_element_type=jnp.float32)
    )
    mixed = stream_out.astype(jnp.bfloat16)
    grad_three = cotangent.astype(jnp.float32)
    grad_w_down, grad_act = out_backward(activated, w_down, grad_three)
    _, gelu_pull = jax.vjp(jax.nn.gelu, hidden_pre)
    grad_pre = gelu_pull(grad_act)[0].astype(jnp.bfloat16)
    grad_w_up = jnp.einsum(
        "fcsd,fcsh->dh", gathered_ff, grad_pre, preferred_element_type=jnp.float32
    )
    grad_part, grad_gain_ff = norm_backward(
        jnp.einsum("fcsh,dh->fcsd", grad_pre, w_up, preferred_element_type=jnp.float32),
        stream_two,
        gain_ff,
    )
    grad_two = grad_three + grad_part
    grad_w_out_tm, grad_att_tm = out_backward(attended_tm, w_out_time, grad_two)
    grad_att_tm = grad_att_tm.astype(jnp.bfloat16)
    grad_scores, soft_weights = time_probs(
        queries_tm, keys_every, values_every, log_norm_tm, grad_att_tm, my_frame
    )
    grad_q_tm = time_query_grads(grad_scores, keys_every)
    grad_k_part, grad_v_part = time_key_grads(grad_scores, soft_weights, queries_tm, grad_att_tm)
    summed_terms = lax.psum_scatter(
        jnp.concatenate([grad_k_part, grad_v_part], axis=-1).astype(jnp.bfloat16),
        "frames",
        scatter_dimension=0,
        tiled=True,
    ).astype(jnp.float32)
    feature_count = queries_tm.shape[-1]
    grad_k_tm = summed_terms[..., :feature_count].astype(jnp.bfloat16)
    grad_v_tm = summed_terms[..., feature_count:].astype(jnp.bfloat16)
    grad_w_qkv_tm, grad_part, grad_gain_tm = qkv_backward(
        gathered_tm, w_qkv_time, grad_q_tm, grad_k_tm, grad_v_tm, stream_one, gain_tm
    )
    grad_one = grad_two + grad_part
    grad_w_out_sp, grad_att_sp = out_backward(attended_sp, w_out_space, grad_one)
    grad_q_sp, grad_k_sp, grad_v_sp = space_backward(
        queries_sp, keys_sp, values_sp, log_norm_sp, grad_att_sp.astype(jnp.bfloat16)
    )
    grad_w_qkv_sp, grad_part, grad_gain_sp = qkv_backward(
        gathered_sp, w_qkv_space, grad_q_sp, grad_k_sp, grad_v_sp, stream_zero, gain_sp
    )
    grad_zero = grad_one + grad_part
    grad_tab = jnp.einsum("fck,fcd->kd", one_hot, jnp.sum(grad_zero, axis=2))
    weight_totals = (
        lax.psum(grad_w_qkv_sp.astype(jnp.bfloat16), "frames").astype(jnp.float32),
        lax.psum(grad_w_out_sp.astype(jnp.bfloat16), "frames").astype(jnp.float32),
        lax.psum(grad_w_qkv_tm.astype(jnp.bfloat16), "frames").astype(jnp.float32),
        lax.psum(grad_w_out_tm.astype(jnp.bfloat16), "frames").astype(jnp.float32),
        lax.psum(grad_w_up.astype(jnp.bfloat16), "frames").astype(jnp.float32),
        lax.psum(grad_w_down.astype(jnp.bfloat16), "frames").astype(jnp.float32),
    )
    small_totals = lax.psum(
        (grad_tab, grad_gain_sp, grad_gain_tm, grad_gain_ff), ("tensor", "frames")
    )
    return (
        mixed,
        grad_zero,
        small_totals[0],
        small_totals[1],
        small_totals[2],
        small_totals[3],
        weight_totals[0],
        weight_totals[1],
        weight_totals[2],
        weight_totals[3],
        weight_totals[4],
        weight_totals[5],
    )


def solution(mesh):
    return jax.shard_map(
        body,
        mesh=mesh,
        in_specs=(
            P("frames", None, "tensor", None),
            P("frames", None),
            P(),
            P(),
            P(),
            P(),
            P(None, None, "tensor"),
            P("tensor", None),
            P(None, None, "tensor"),
            P("tensor", None),
            P(None, "tensor"),
            P("tensor", None),
            P("frames", None, "tensor", None),
        ),
        out_specs=(
            P("frames", None, "tensor", None),
            P("frames", None, "tensor", None),
            P(),
            P(),
            P(),
            P(),
            P(None, None, "tensor"),
            P("tensor", None),
            P(None, None, "tensor"),
            P("tensor", None),
            P(None, "tensor"),
            P("tensor", None),
        ),
        check_vma=False,
    )
```

profile of v0, /device:TPU:0, one launch (start us, length us, event | category | flops | bytes accessed | tf_op | source)
XLA Modules:
  0.0 1636.9 jit_solution(5795226820691867186)
XLA Ops:
  15.1 37.3 %all-gather.11.cloned.1.call-done = bf16[1,8,256,1024]{3,2,1,0:T(8,128)(2,1)} async-done(((bf16[1,8,64,1024]{3,2,1,0:T(8,128)(2,1)}), bf16[1,8,256,1024]{3,2,1,0:T(8,128)(2,1)}) %all-gather.11.cloned.1.call-update) | async-done | bytes 4194320 | tf_op jit(solution)/shard_map/all_gather | solution.py:18
  71.2 71.2 %reduce-scatter.8.cloned.1.call-done = f32[1,8,64,1024]{3,2,1,0:T(8,128)} async-done(((f32[1,8,256,1024]{3,2,1,0:T(8,128)}), f32[1,8,64,1024]{3,2,1,0:T(8,128)}) %reduce-scatter.8.cloned.1.call-update) | async-done | bytes 2097168 | tf_op jit(solution)/shard_map/reduce_scatter | solution.py:22
  147.5 34.1 %all-gather.13.cloned.1.call-done = bf16[1,8,256,1024]{3,2,1,0:T(8,128)(2,1)} async-done(((bf16[1,8,64,1024]{3,2,1,0:T(8,128)(2,1)}), bf16[1,8,256,1024]{3,2,1,0:T(8,128)(2,1)}) %all-gather.13.cloned.1.call-update) | async-done | bytes 4194320 | tf_op jit(solution)/shard_map/all_gather | solution.py:18
  195.7 121.1 %all-gather.25.cloned.1.call-done = bf16[8,8,256,1,256]{4,2,3,1,0:T(8,128)(2,1)} async-done(((bf16[1,8,256,1,256]{4,2,3,1,0:T(8,128)(2,1)}), bf16[8,8,256,1,256]{4,2,3,1,0:T(8,128)(2,1)}) %all-gather.25.cloned.1.call-update) | async-done | bytes 8388624 | tf_op jit(solution)/shard_map/all_gather | solution.py:209
  316.8 11.6 copy.184
  336.3 106.4 %all-gather.23.cloned.1.call-done = bf16[8,8,256,1,256]{4,2,3,1,0:T(8,128)(2,1)} async-done(((bf16[1,8,256,1,256]{4,2,3,1,0:T(8,128)(2,1)}), bf16[8,8,256,1,256]{4,2,3,1,0:T(8,128)(2,1)}) %all-gather.23.cloned.1.call-update) | async-done | bytes 8388624 | tf_op jit(solution)/shard_map/all_gather | solution.py:210
  442.7 11.4 copy.183
  466.3 69.4 %reduce-scatter.10.cloned.1.call-done = f32[1,8,64,1024]{3,2,1,0:T(8,128)} async-done(((f32[1,8,256,1024]{3,2,1,0:T(8,128)}), f32[1,8,64,1024]{3,2,1,0:T(8,128)}) %reduce-scatter.10.cloned.1.call-update) | async-done | bytes 2097168 | tf_op jit(solution)/shard_map/reduce_scatter | solution.py:22
  541.7 33.7 %all-gather.15.cloned.1.call-done = bf16[1,8,256,1024]{3,2,1,0:T(8,128)(2,1)} async-done(((bf16[1,8,64,1024]{3,2,1,0:T(8,128)(2,1)}), bf16[1,8,256,1024]{3,2,1,0:T(8,128)(2,1)}) %all-gather.15.cloned.1.call-update) | async-done | bytes 4194320 | tf_op jit(solution)/shard_map/all_gather | solution.py:18
  584.4 27.1 %all-gather.17.cloned.1.call-done = bf16[1,8,256,1024]{3,2,1,0:T(8,128)(2,1)} async-done(((bf16[1,8,64,1024]{3,2,1,0:T(8,128)(2,1)}), bf16[1,8,256,1024]{3,2,1,0:T(8,128)(2,1)}) %all-gather.17.cloned.1.call-update) | async-done | bytes 4194320 | tf_op jit(solution)/shard_map/all_gather | solution.py:26
  611.5 12.5 fusion.6
  632.3 44.6 %reduce-scatter.14.cloned.1.call-done = bf16[1,8,64,1024]{3,2,1,0:T(8,128)(2,1)} async-done(((bf16[1,8,256,1024]{3,2,1,0:T(8,128)(2,1)}), bf16[1,8,64,1024]{3,2,1,0:T(8,128)(2,1)}) %reduce-scatter.14.cloned.1.call-update) | async-done | bytes 1048592 | tf_op jit(solution)/shard_map/reduce_scatter | solution.py:30
  682.6 34.4 %all-gather.19.cloned.1.call-done = bf16[1,8,256,1024]{3,2,1,0:T(8,128)(2,1)} async-done(((bf16[1,8,64,1024]{3,2,1,0:T(8,128)(2,1)}), bf16[1,8,256,1024]{3,2,1,0:T(8,128)(2,1)}) %all-gather.19.cloned.1.call-update) | async-done | bytes 4194320 | tf_op jit(solution)/shard_map/all_gather | solution.py:26
  720.6 11.9 multiply_reduce_fusion.1
  732.5 11.6 copy.124
  750.3 11.4 copy.123
  761.7 13.6 pad_maximum_fusion
  782.7 275.5 %reduce-scatter.16.cloned.1.call-done = bf16[1,8,256,512]{3,2,1,0:T(8,128)(2,1)} async-done(((bf16[8,8,256,512]{3,2,1,0:T(8,128)(2,1)}), bf16[1,8,256,512]{3,2,1,0:T(8,128)(2,1)}) %reduce-scatter.16.cloned.1.call-update) | async-done | bytes 2097168 | tf_op jit(solution)/shard_map/reduce_scatter | solution.py:245
  1067.6 12.4 convolution_bitcast_fusion
  1080.1 29.6 %reduce-scatter.18.cloned.1.call-done = bf16[1,8,64,1024]{3,2,1,0:T(8,128)(2,1)} async-done(((bf16[1,8,256,1024]{3,2,1,0:T(8,128)(2,1)}), bf16[1,8,64,1024]{3,2,1,0:T(8,128)(2,1)}) %reduce-scatter.18.cloned.1.call-update) | async-done | bytes 1048592 | tf_op jit(solution)/shard_map/reduce_scatter | solution.py:30
  1112.3 71.9 %reduce-scatter.12.cloned.1.call-done = f32[1,8,64,1024]{3,2,1,0:T(8,128)} async-done(((f32[1,8,256,1024]{3,2,1,0:T(8,128)}), f32[1,8,64,1024]{3,2,1,0:T(8,128)}) %reduce-scatter.12.cloned.1.call-update) | async-done | bytes 2097168 | tf_op jit(solution)/shard_map/reduce_scatter | solution.py:22
  1261.4 266.3 %all-reduce.4.cloned.1.call-done = (bf16[1024,3,256]{2,0,1:T(8,128)(2,1)}, bf16[256,1024]{1,0:T(8,128)(2,1)}, bf16[1024,3,256]{2,0,1:T(8,128)(2,1)}, bf16[256,10...) async-done(((bf16[1024,3,256]{2,0,1:T(8,128)(2,1)}, bf16[256,1024]{1,0:T(8,128)(2,1)}, bf16[1024,3,256]{2,0,1:T(8,128)(2,1)}, ...) | async-done | bytes 8388624 | tf_op jit(solution)/shard_map/psum | solution.py:268
  1532.0 42.0 %reduce-scatter.20.cloned.1.call-done = bf16[1,8,64,1024]{3,2,1,0:T(8,128)(2,1)} async-done(((bf16[1,8,256,1024]{3,2,1,0:T(8,128)(2,1)}), bf16[1,8,64,1024]{3,2,1,0:T(8,128)(2,1)}) %reduce-scatter.20.cloned.1.call-update) | async-done | bytes 1048592 | tf_op jit(solution)/shard_map/reduce_scatter | solution.py:30
  1589.6 40.3 %all-reduce = (f32[8,1024]{1,0:T(8,128)}, f32[1024]{0:T(1024)}, f32[1024]{0:T(1024)}, f32[1024]{0:T(1024)}) all-reduce(f32[8,1024]{1,0:T(8,128)S(1)} %fusion.97, f32[1024]{0:T(1024)S(1)} %get-tuple-element.16, f32[1024]{0:T(1024)S(1)} %copy-done.51, f32[1024]{0:T(1024)S(1)} %copy-done.50), channel_id=1, replica_groups=mesh['tensor'=4,'frames'=8] {'tensor','frames'}, use_global_device_ids=true, to_apply=%region_21.22 | all-reduce | flops 11264 | bytes 90112 | tf_op jit(solution)/shard_map/psum | solution.py:275
  (240 shorter events, 220.5 us)
Async XLA Ops:
  7.2 568.2 %copy-start = (bf16[1024,1024]{1,0:T(8,128)(2,1)S(1)}, bf16[1024,1024]{1,0:T(8,128)(2,1)}, u32[]{:S(2)}) copy-start(bf16[1024,1024]{1,0:T(8,128)(2,1)} %param.23) | copy-start | bytes 6291460
  7.2 45.2 %all-gather.11.cloned.1.call-start = ((), (), s32[]{:S(2)}) async-start(), calls=%async_computation.7 | async-start | bytes 5242880 | tf_op jit(solution)/shard_map/all_gather | solution.py:18
  9.7 132.8 %copy-start.28 = (f32[8,1024]{1,0:T(8,128)}, f32[8,1024]{1,0:T(8,128)S(1)}, u32[]{:S(2)}) copy-start(f32[8,1024]{1,0:T(8,128)S(1)} %multiply_reduce_fusion.10) | copy-start | bytes 98308
  15.0 127.4 %reduce-scatter.8.cloned.1.call-start = ((), (), s32[]{:S(2)}) async-start(), calls=%async_computation.8 | async-start | bytes 10485760 | tf_op jit(solution)/shard_map/reduce_scatter | solution.py:22
  70.6 111.1 %all-gather.13.cloned.1.call-start = ((), (), s32[]{:S(2)}) async-start(), calls=%async_computation.9 | async-start | bytes 5242880 | tf_op jit(solution)/shard_map/all_gather | solution.py:18
  147.0 169.8 %all-gather.25.cloned.1.call-start = ((), (), s32[]{:S(2)}) async-start(), calls=%async_computation.21 | async-start | bytes 9437184 | tf_op jit(solution)/shard_map/all_gather | solution.py:209
  191.7 251.0 %all-gather.23.cloned.1.call-start = ((), (), s32[]{:S(2)}) async-start(), calls=%async_computation.20 | async-start | bytes 9437184 | tf_op jit(solution)/shard_map/all_gather | solution.py:210
  194.0 341.6 %reduce-scatter.10.cloned.1.call-start = ((), (), s32[]{:S(2)}) async-start(), calls=%async_computation.10 | async-start | bytes 10485760 | tf_op jit(solution)/shard_map/reduce_scatter | solution.py:22
  465.6 109.8 %all-gather.15.cloned.1.call-start = ((), (), s32[]{:S(2)}) async-start(), calls=%async_computation.11 | async-start | bytes 5242880 | tf_op jit(solution)/shard_map/all_gather | solution.py:18
  540.8 70.7 %all-gather.17.cloned.1.call-start = ((), (), s32[]{:S(2)}) async-start(), calls=%async_computation.13 | async-start | bytes 5242880 | tf_op jit(solution)/shard_map/all_gather | solution.py:26
  541.5 135.4 %reduce-scatter.14.cloned.1.call-start = ((), (), s32[]{:S(2)}) async-start(), calls=%async_computation.14 | async-start | bytes 5242880 | tf_op jit(solution)/shard_map/reduce_scatter | solution.py:30
  632.3 84.7 %all-gather.19.cloned.1.call-start = ((), (), s32[]{:S(2)}) async-start(), calls=%async_computation.15 | async-start | bytes 5242880 | tf_op jit(solution)/shard_map/all_gather | solution.py:26
  682.3 375.9 %reduce-scatter.16.cloned.1.call-start = ((), (), s32[]{:S(2)}) async-start(), calls=%async_computation.16 | async-start | bytes 18874368 | tf_op jit(solution)/shard_map/reduce_scatter | solution.py:245
  775.3 334.4 %reduce-scatter.18.cloned.1.call-start = ((), (), s32[]{:S(2)}) async-start(), calls=%async_computation.17 | async-start | bytes 5242880 | tf_op jit(solution)/shard_map/reduce_scatter | solution.py:30
  782.7 283.3 %copy-start.30 = (bf16[1,8,256,1,256]{4,2,3,1,0:T(8,128)(2,1)}, bf16[1,8,256,1,256]{4,2,3,1,0:T(8,128)(2,1)S(1)}, u32[]{:S(2)}) copy-start(bf16[1,8,256,1,256]{4,2,3,1,0:T(8,128)(2,1)S(1)} %copy.125) | copy-start | bytes 3145732
  1066.0 118.2 %reduce-scatter.12.cloned.1.call-start = ((), (), s32[]{:S(2)}) async-start(), calls=%async_computation.12 | async-start | bytes 10485760 | tf_op jit(solution)/shard_map/reduce_scatter | solution.py:22
  1080.0 143.7 %all-gather.21.cloned.1.call-start = ((), (), s32[]{:S(2)}) async-start(), calls=%async_computation.18 | async-start | bytes 5242880 | tf_op jit(solution)/shard_map/all_gather | solution.py:26
  1189.1 338.6 %all-reduce.4.cloned.1.call-start = ((), (), s32[]{:S(2)}) async-start(), calls=%async_computation.22 | async-start | bytes 16777216 | tf_op jit(solution)/shard_map/psum | solution.py:268
  1253.5 320.4 %reduce-scatter.20.cloned.1.call-start = ((), (), s32[]{:S(2)}) async-start(), calls=%async_computation.19 | async-start | bytes 5242880 | tf_op jit(solution)/shard_map/reduce_scatter | solution.py:30
  1261.4 312.6 %copy-start.8 = (bf16[1,8,64,1024]{3,2,1,0:T(8,128)(2,1)S(1)}, bf16[1,8,64,1024]{3,2,1,0:T(8,128)(2,1)}, u32[]{:S(2)}) copy-start(bf16[1,8,64,1024]{3,2,1,0:T(8,128)(2,1)} %param.13) | copy-start | bytes 3145732
  1261.4 312.6 %copy-start.29 = (f32[8,1024]{1,0:T(8,128)S(1)}, f32[8,1024]{1,0:T(8,128)}, u32[]{:S(2)}) copy-start(f32[8,1024]{1,0:T(8,128)} %copy-done.28) | copy-start | bytes 98308
  1261.4 312.6 %copy-start.45 = (f32[1024]{0:T(1024)S(1)}, f32[1024]{0:T(1024)}, u32[]{:S(2)}) copy-start(f32[1024]{0:T(1024)} %copy-done.44) | copy-start | bytes 12292
  1261.4 312.6 %copy-start.47 = (f32[8,64]{1,0:T(8,128)S(1)}, f32[8,64]{1,0:T(8,128)}, u32[]{:S(2)}) copy-start(f32[8,64]{1,0:T(8,128)} %copy-done.46) | copy-start | bytes 6148
  1261.4 315.0 %copy-start.49 = (f32[8,64]{1,0:T(8,128)S(1)}, f32[8,64]{1,0:T(8,128)}, u32[]{:S(2)}) copy-start(f32[8,64]{1,0:T(8,128)} %copy-done.48) | copy-start | bytes 6148
  (56 other events, 733.5 us)
Sparse Core Ops, SparseCore 0:
  15.2 37.1 all-gather.10
  70.7 71.7 reduce-scatter.7
  147.2 34.4 all-gather.12
  191.8 124.9 all-gather.24
  319.6 123.1 all-gather.22
  465.7 69.9 reduce-scatter.9
  540.9 34.4 all-gather.14
  577.0 34.4 all-gather.16
  632.4 44.4 reduce-scatter.13
  682.5 34.4 all-gather.18
  775.4 282.7 reduce-scatter.15
  1066.2 43.5 reduce-scatter.17
  1112.5 71.6 reduce-scatter.11
  1189.2 34.4 all-gather.20
  1253.6 274.0 all-reduce.3
  1530.7 43.2 reduce-scatter.19
where the time goes:
time: 1650 us; the launch traced here: 1640 us
  waiting for transfers between devices  1270 us (77%)
  matrix products  130 us (8%)
  other arithmetic  103 us (6%)
  local copies, waits for them, and re-layouts  74.5 us (5%)
  blocking collectives  40.3 us (2%)
    reduce_scatter x1, waiting for transfers between devices, body(): lax.psum_scatter(jnp.concatenate([grad_k_part, grad_v_part], axis=-1).ast...  276 us
    psum x1, waiting for transfers between devices, body(): lax.psum(grad_w_qkv_sp.astype(jnp.bfloat16), 'frames').astype(jnp.float32)  266 us
    reduce_scatter x3, waiting for transfers between devices, collect(): return lax.psum_scatter(values, 'tensor', scatter_dimension=2, tiled=True)  213 us
    all_gather x1, waiting for transfers between devices, body(): lax.all_gather(keys_tm, 'frames', axis=0, tiled=True)  121 us
    reduce_scatter x3, waiting for transfers between devices, collect_back(): lax.psum_scatter(values.astype(jnp.bfloat16), 'tensor', scatter_dimension...  116 us
    all_gather x1, waiting for transfers between devices, body(): lax.all_gather(values_tm, 'frames', axis=0, tiled=True)  106 us
    all_gather x3, waiting for transfers between devices, spread(): return lax.all_gather(values, 'tensor', axis=2, tiled=True)  105 us
    all_gather x3, waiting for transfers between devices, spread_back(): return lax.all_gather(values, 'tensor', axis=2, tiled=True)  67.7 us
  transfers between devices with their start and end apart: 16, of which 16 were waited for; matrix products, arithmetic and copies ran while one was open for 6% of the time, Pallas kernels for 0%

commit v1 on v0

v1 whole, which is shorter than its diff:
```python
import functools

import jax
import jax.numpy as jnp
from jax import lax
from jax.experimental import pallas as pl
from jax.experimental.pallas import tpu as pltpu
from jax.sharding import PartitionSpec as P

HD = 64
EPS = 1e-06
BF = jnp.bfloat16
F32 = jnp.float32
MESH = pl.DeviceIdType.MESH
LIMIT = 63 * 1024 * 1024
LAG = 5
GAP = 2
CHUNKS = 8


def dot(left, right, contract):
    return lax.dot_general(left, right, ((contract[:1], contract[1:]), ((), ())), preferred_element_type=F32)


def norm_parts(values):
    factor = lax.rsqrt(jnp.mean(values * values, axis=-1, keepdims=True) + EPS)
    return values * factor, factor


def norm_backward(grad_normed, stream, gain_vec):
    unit, factor = norm_parts(stream)
    scaled = grad_normed * gain_vec
    grad_stream = (scaled - unit * jnp.mean(scaled * unit, axis=-1, keepdims=True)) * factor
    return grad_stream, jnp.sum(grad_normed * unit, axis=0, keepdims=True)


def head_mask(rows, width, head):
    lane = lax.broadcasted_iota(jnp.int32, (rows, width), 1)
    return (lane >= head * HD) & (lane < (head + 1) * HD)


def visible(rows, frames, query_dim=0):
    part = rows // 4
    spots = part // frames
    row = lax.broadcasted_iota(jnp.int32, (rows, rows), query_dim)
    col = lax.broadcasted_iota(jnp.int32, (rows, rows), 1 - query_dim)
    same_part = row // part == col // part
    same_spot = row % spots == col % spots
    earlier = (col % part) // spots <= (row % part) // spots
    return same_part & same_spot & earlier


def block_probs(queries, keys_in, seen):
    scores = dot(queries, keys_in, (1, 1))
    if seen is not None:
        scores = jnp.where(seen[...] > 0, scores, -1e30)
    raised = jnp.exp(scores - jnp.max(scores, axis=-1, keepdims=True))
    return raised * (1.0 / jnp.sum(raised, axis=-1, keepdims=True))


def attend(queries, keys_in, values, seen):
    rows, width = queries.shape
    total = jnp.zeros((rows, width), F32)
    queries = queries * BF(HD ** (-0.5))
    for head in range(width // HD):
        mine = head_mask(rows, width, head)
        probs = block_probs(jnp.where(mine, queries, 0), keys_in, seen)
        total = total + dot(probs.astype(BF), jnp.where(mine, values, 0), (1, 0))
    return total.astype(BF)


def attend_back(queries, keys_in, values, grad_att, seen):
    rows, width = queries.shape
    zero = jnp.zeros((rows, width), F32)
    grad_q, grad_k, grad_v = zero, zero, zero
    scale = BF(HD ** (-0.5))
    queries = queries * scale
    scaled_keys = keys_in * scale
    for head in range(width // HD):
        mine = head_mask(rows, width, head)
        my_queries = jnp.where(mine, queries, 0)
        my_grad = jnp.where(mine, grad_att, 0)
        scores = dot(keys_in, my_queries, (1, 1))
        if seen is not None:
            scores = jnp.where(seen[...] > 0, scores, -1e30)
        raised = jnp.exp(scores - jnp.max(scores, axis=0, keepdims=True))
        probs = raised * (1.0 / jnp.sum(raised, axis=0, keepdims=True))
        grad_probs = dot(values, my_grad, (1, 1))
        row_dot = jnp.sum(grad_probs * probs, axis=0, keepdims=True)
        grad_scores = (probs * (grad_probs - row_dot)).astype(BF)
        grad_q = grad_q + dot(grad_scores, jnp.where(mine, scaled_keys, 0), (0, 0))
        grad_k = grad_k + dot(grad_scores, my_queries, (1, 0))
        grad_v = grad_v + dot(probs.astype(BF), my_grad, (1, 0))
    return grad_q.astype(BF), grad_k.astype(BF), grad_v.astype(BF)


class Group:
    def __init__(self, frames=1, all_frames=False):
        me = lax.axis_index("tensor")
        self.x, self.c = me // 2, me % 2
        self.me = me
        self.chip_peer = 2 * (1 - self.x) + self.c
        self.core_peer = 2 * self.x + 1 - self.c
        self.levels = frames.bit_length() - 1
        self.bits, self.partners = [], []
        self.frames, self.all_frames = frames, all_frames
        self.frame = frame = lax.axis_index("frames")
        for level in range(self.levels):
            bit = (frame // 2**level) % 2
            self.bits.append(bit)
            self.partners.append(frame + (1 - 2 * bit) * 2**level)

    def everyone(self):
        return [("tensor", self.chip_peer), ("tensor", self.core_peer)] + [
            ("frames", partner) for partner in self.partners
        ]

    def other_frame(self, distance):
        return (self.frame + distance) % self.frames

    def meet(self):
        barrier = pltpu.get_barrier_semaphore()
        peers = self.everyone()
        if self.all_frames:
            peers = peers[:2] + [("frames", self.other_frame(far)) for far in range(1, self.frames)]
        for axis, peer in peers:
            pl.semaphore_signal(barrier, inc=1, device_id={axis: peer}, device_id_type=MESH)
        pl.semaphore_wait(barrier, len(peers))


def remote(src, dst, sems, kind, block, peer, axis="tensor"):
    return pltpu.make_async_remote_copy(
        src_ref=src,
        dst_ref=dst,
        send_sem=sems.at[0, kind, block],
        recv_sem=sems.at[1, kind, block],
        device_id={axis: peer},
        device_id_type=MESH,
    )


class Gather:
    def __init__(self, group, whole, sems):
        self.group, self.whole, self.sems = group, whole, sems

    def copy(self, kind, block):
        g = self.group
        quarter = self.whole.at[block, g.chip_peer if kind == 2 else g.me]
        return remote(quarter, quarter, self.sems, kind, block, g.chip_peer if kind == 0 else g.core_peer)

    def start(self, block):
        self.copy(0, block).start()
        self.copy(1, block).start()

    def forward(self, block):
        self.copy(0, block).wait_recv()
        self.copy(2, block).start()

    def arrive(self, block):
        self.copy(1, block).wait_recv()
        self.copy(2, block).wait_recv()

    def sent(self, block):
        for kind in range(3):
            self.copy(kind, block).wait_send()

    @staticmethod
    def scratch(blocks):
        return pltpu.SemaphoreType.DMA((2, 3, blocks))


class Scatter:
    def __init__(self, group, kept, near_out, near_in, far_out, far_in, sems):
        self.group, self.kept, self.sems = group, kept, sems
        self.near_out, self.near_in, self.far_out, self.far_in = near_out, near_in, far_out, far_in
        self.slots, self.blocks = near_out.shape[0], sems.shape[2]

    def near(self, block):
        slot = block % self.slots
        return remote(self.near_out.at[slot], self.near_in.at[slot], self.sems, 0, block, self.group.core_peer)

    def far(self, block):
        slot = block % self.slots
        return remote(self.far_out.at[slot], self.far_in.at[slot], self.sems, 1, block, self.group.chip_peer)

    def free(self, block):
        if self.blocks > self.slots:

            @pl.when(block >= self.slots)
            def _():
                self.near(block - self.slots).wait_send()
                self.far(block - self.slots).wait_send()

    def put(self, block, values, more=False):
        slot = block % self.slots
        for x in range(2):
            first, second = (values[(2 * x + c) * self.part : (2 * x + c + 1) * self.part] for c in range(2))
            own = jnp.where(self.group.c == 0, first, second)
            given = jnp.where(self.group.c == 0, second, first)
            if more:
                own = own + self.kept[slot, x]
                given = given + self.near_out[slot, x].astype(F32)
            self.kept[slot, x] = own
            self.near_out[slot, x] = given.astype(BF)

    def send(self, block, values, more=False):
        self.put(block, values, more)
        self.near(block).start()

    @property
    def part(self):
        return self.kept.shape[2]

    def cross(self, block):
        x, slot = 1 - self.group.x, block % self.slots
        self.near(block).wait_recv()
        self.far_out[slot] = (self.kept[slot, x] + self.near_in[slot, x].astype(F32)).astype(BF)
        self.far(block).start()

    def take(self, block):
        x, slot = self.group.x, block % self.slots
        self.far(block).wait_recv()
        return self.kept[slot, x] + self.near_in[slot, x].astype(F32) + self.far_in[slot].astype(F32)

    def finish(self):
        def sent(block, carry):
            self.near(block).wait_send()
            self.far(block).wait_send()
            return carry

        lax.fori_loop(self.blocks - self.slots, self.blocks, sent, 0)

    @staticmethod
    def scratch(blocks, slots, part, width):
        return [
            pltpu.VMEM((slots, 2, part, width), F32),
            pltpu.VMEM((slots, 2, part, width), BF),
            pltpu.VMEM((slots, 2, part, width), BF),
            pltpu.VMEM((slots, part, width), BF),
            pltpu.VMEM((slots, part, width), BF),
            pltpu.SemaphoreType.DMA((2, 2, blocks)),
        ]


def packed_shape(blocks, frames, part, width):
    spots = part // frames
    cuts = max(1, 16 // spots)
    return (blocks, frames, cuts * spots, width // cuts)


def pack(values, frames):
    rows, width = values.shape
    spots = rows // frames
    cuts = max(1, 16 // spots)
    wide = width // cuts
    return [
        jnp.concatenate(
            [values[frame * spots : (frame + 1) * spots, k * wide : (k + 1) * wide] for k in range(cuts)], axis=0
        )
        for frame in range(frames)
    ]


def unpack(packed, width):
    frames, rows, wide = packed.shape
    cuts = width // wide
    spots = rows // cuts
    packed = packed.astype(F32)
    return jnp.concatenate(
        [
            jnp.concatenate([packed[frame, k * spots : (k + 1) * spots] for k in range(cuts)], axis=1)
            for frame in range(frames)
        ],
        axis=0,
    )


class Exchange:
    def __init__(self, group, stage, landing, sems):
        self.group, self.stage, self.landing, self.sems = group, stage, landing, sems

    def copy(self, block, far):
        g = self.group
        other = g.other_frame(far)
        return remote(
            self.stage.at[block, other], self.landing.at[block, g.frame], self.sems, far - 1, block, other, "frames"
        )

    def push(self, block, values):
        frames = self.group.frames
        for frame, piece in enumerate(pack(values, frames)):
            self.stage[block, frame] = piece.astype(BF)
        self.landing[block, self.group.frame] = self.stage[block, self.group.frame]
        for far in range(1, frames):
            self.copy(block, far).start()

    def arrive(self, block):
        for far in range(1, self.group.frames):
            self.copy(block, far).wait_recv()

    def sent(self, block):
        for far in range(1, self.group.frames):
            self.copy(block, far).wait_send()

    @staticmethod
    def scratch(shape):
        return [pltpu.VMEM(shape, BF), pltpu.SemaphoreType.DMA((2, shape[1] - 1, shape[0]))]


class Reduce:
    def __init__(self, group_size, slack, load, group, source, result, stage, landing, sems):
        self.group_size, self.slack, self.load = group_size, slack, load
        self.group, self.source, self.result = group, source, result
        self.stage, self.landing, self.sems = stage, landing, sems
        self.chunks, self.pieces = result.shape[:2]
        self.levels = group.levels

    def half(self, level):
        return self.pieces >> (level + 1)

    def choice(self, chunk, level, normal):
        turned = 1 - (chunk + self.chunks - 1) // self.chunks
        return normal[level] + turned * (normal[(level + 1) % self.levels] - normal[level])

    def bit(self, chunk, level):
        return self.choice(chunk, level, self.group.bits)

    def partner(self, chunk, level):
        return self.choice(chunk, level, self.group.partners)

    def offset(self, chunk, level):
        return sum((self.bit(chunk, k) * self.half(k) for k in range(level)), 0)

    def place(self, level):
        return pl.ds(self.pieces - (self.pieces >> level), self.half(level))

    def down(self, chunk, level):
        place = self.place(level)
        return remote(
            self.stage.at[chunk, place],
            self.landing.at[chunk, place],
            self.sems,
            level,
            chunk,
            self.partner(chunk, level),
            "frames",
        )

    def up(self, chunk, level):
        done = self.result.at[chunk, pl.ds(self.offset(chunk, level + 1), self.half(level))]
        return remote(done, done, self.sems, self.levels + level, chunk, self.partner(chunk, level), "frames")

    def put(self, chunk, level):
        half = self.half(level)
        given = self.offset(chunk, level) + (1 - self.bit(chunk, level)) * half
        self.stage[chunk, self.place(level)] = self.source[chunk, pl.ds(given, half)].astype(BF)
        self.down(chunk, level).start()

    def add(self, chunk, level):
        self.down(chunk, level).wait_recv()
        kept = pl.ds(self.offset(chunk, level + 1), self.half(level))
        self.source[chunk, kept] = self.source[chunk, kept] + self.landing[chunk, self.place(level)].astype(F32)

    def advance(self, chunk, turn):
        levels = self.levels
        if turn == 0:
            if self.load is not None:
                self.load.wait(chunk)
            self.put(chunk, 0)
        elif turn < levels:
            self.add(chunk, turn - 1)
            self.put(chunk, turn)
        elif turn == levels:
            self.add(chunk, levels - 1)
            mine = pl.ds(self.offset(chunk, levels), 1)
            self.result[chunk, mine] = self.source[chunk, mine].astype(BF)
            self.up(chunk, levels - 1).start()
        else:
            self.up(chunk, 2 * levels - turn).wait_recv()
            self.up(chunk, 2 * levels - turn - 1).start()

    def tick(self, time):
        for turn in range(2 * self.levels):
            first = time - turn - (self.slack if turn else 0)

            @pl.when((first >= 0) & (first < self.chunks // self.group_size))
            def _():
                for k in range(self.group_size):
                    self.advance(first * self.group_size + k, turn)

    def last(self):
        return self.chunks // self.group_size + 2 * self.levels - 2 + self.slack

    def finish(self):
        def done(chunk, carry):
            self.up(chunk, 0).wait_recv()
            for level in range(self.levels):
                self.down(chunk, level).wait_send()
                self.up(chunk, level).wait_send()
            return carry

        lax.fori_loop(0, self.chunks, done, 0)

    @staticmethod
    def scratch(shape):
        chunks, pieces, part, width = shape
        levels = pieces.bit_length() - 1
        return [
            pltpu.VMEM((chunks, pieces - 1, part, width), BF),
            pltpu.VMEM((chunks, pieces - 1, part, width), BF),
            pltpu.SemaphoreType.DMA((2, 2 * levels, chunks)),
        ]


class SmallSum:
    def __init__(self, group, total, out, landing, sems):
        self.peers = group.everyone()
        self.total, self.out, self.landing, self.sems = total, out, landing, sems

    def copy(self, turn):
        axis, peer = self.peers[turn]
        return remote(self.out.at[turn], self.landing.at[turn], self.sems, 0, turn, peer, axis)

    def tick(self, time):
        for turn in range(len(self.peers) + 1):

            @pl.when(time == turn)
            def _():
                if turn > 0:
                    self.copy(turn - 1).wait_recv()
                    self.total[...] += self.landing[turn - 1]
                if turn < len(self.peers):
                    self.out[turn] = self.total[...]
                    self.copy(turn).start()

    def last(self):
        return len(self.peers)

    def finish(self):
        for turn in range(len(self.peers)):
            self.copy(turn).wait_send()

    @staticmethod
    def scratch(peers, shape):
        return [
            pltpu.VMEM((peers,) + shape, F32),
            pltpu.VMEM((peers,) + shape, F32),
            pltpu.SemaphoreType.DMA((2, 1, peers)),
        ]


class Bulk:
    def __init__(self, group, source, landing, sems, own_sem):
        self.group, self.source, self.landing, self.sems = group, source, landing, sems
        frame = group.frame
        self.own = pltpu.make_async_copy(source.at[frame], landing.at[frame], own_sem)

    def copy(self, far):
        other = self.group.other_frame(far)
        return remote(
            self.source.at[other], self.landing.at[self.group.frame], self.sems, 0, far - 1, other, "frames"
        )

    def start(self):
        self.own.start()
        for far in range(1, self.group.frames):
            self.copy(far).start()

    def finish(self):
        self.own.wait()
        for far in range(1, self.group.frames):
            self.copy(far).wait()

    @staticmethod
    def scratch(frames):
        return [pltpu.SemaphoreType.DMA((2, 1, frames - 1)), pltpu.SemaphoreType.DMA]


class Twice:
    def __init__(self, scatter, before):
        self.scatter, self.before = scatter, before

    def cross(self, pair):
        for k in range(2):
            self.scatter.cross(2 * pair + k + self.before)


class Move:
    def __init__(self, pairs, sems, shift=0):
        self.pairs, self.sems, self.shift = pairs, sems, shift

    def copies(self, block):
        return [
            pltpu.make_async_copy(
                src.at[block % src.shape[0]], dst.at[(block + self.shift) % dst.shape[0]], self.sems.at[k, block]
            )
            for k, (src, dst) in enumerate(self.pairs)
        ]

    def start(self, block):
        for copy in self.copies(block):
            copy.start()

    def wait(self, block):
        for copy in self.copies(block):
            copy.wait()


def pipeline(phases, steps=0, beside=None):
    def step(i, carry):
        for lag in (0, 1, 2, LAG):
            first = 0
            for blocks, gathers, scatters, compute, take in phases:
                block = i - lag - first
                first += blocks

                @pl.when((block >= 0) & (block < blocks))
                def _():
                    if lag == 0:
                        for gather in gathers:
                            gather.forward(block)
                    elif lag == 1:
                        for gather in gathers:
                            gather.arrive(block)
                        compute(block)
                    elif lag == 2:
                        for scatter, before in scatters:
                            scatter.cross(block + before)
                    elif take is not None:
                        take(block)

        if beside is not None:
            beside(i)
        return carry

    lax.fori_loop(0, max(sum(phase[0] for phase in phases) + LAG, steps), step, 0)
    for scatter in {id(scatter): scatter for phase in phases for scatter, _ in phase[2]}.values():
        if isinstance(scatter, Scatter):
            scatter.finish()


def coded_rows(codes_ref, block, actions):
    return (lax.broadcasted_iota(jnp.int32, (actions, 1), 0) == codes_ref[0, block]).astype(F32)


def space_stream(stream_ref, codes_ref, table_ref, block):
    hot = coded_rows(codes_ref, block, table_ref.shape[0])
    added = jnp.sum(hot * table_ref[...].astype(F32), axis=0, keepdims=True)
    return stream_ref[block].astype(F32) + added


def row_of(gain_ref):
    return gain_ref[...].astype(F32)[None]


def attention_block(whole_ref, w_qkv_ref, w_out_ref, qkv_ref, att_ref, seen_ref):
    _, part, width = whole_ref.shape
    normed = whole_ref[...].reshape(4 * part, width)
    for member in range(3):
        qkv_ref[member] = dot(normed, w_qkv_ref[member], (1, 0)).astype(BF)
    att_ref[...] = attend(qkv_ref[0], qkv_ref[1], qkv_ref[2], seen_ref)
    return dot(att_ref[...], w_out_ref[...], (1, 0))


def each_block(blocks, work):
    def one(block, carry):
        work(block)
        return carry

    lax.fori_loop(0, blocks, one, 0)


def call(kernel, name, collective_id, operands, outs, scratch, flops):
    def specs(items):
        return [pl.BlockSpec(memory_space=space) for _, space in items]

    return pl.pallas_call(
        kernel,
        name=name,
        out_shape=[shape for shape, _ in outs],
        in_specs=specs(operands),
        out_specs=specs(outs),
        scratch_shapes=scratch,
        compiler_params=pltpu.CompilerParams(
            collective_id=collective_id, has_side_effects=True, vmem_limit_bytes=LIMIT
        ),
        cost_estimate=pl.CostEstimate(flops=flops, bytes_accessed=16 << 20, transcendentals=0),
    )(*(array for array, _ in operands))


def inside(*items):
    return [(item, pltpu.VMEM) for item in items]


def outside(*items):
    return [(item, pl.ANY) for item in items]


def scalars(item):
    return [(item, pltpu.SMEM)]


def held_like(shapes):
    return [pltpu.VMEM(shape.shape, shape.dtype) for shape in shapes] + [
        pltpu.SemaphoreType.DMA((len(shapes), shapes[0].shape[0]))
    ]


def saved_shapes(blocks, part, width, inner):
    return [
        jax.ShapeDtypeStruct((blocks, 4, part, width), BF),
        jax.ShapeDtypeStruct((blocks, 3, 4 * part, inner), BF),
        jax.ShapeDtypeStruct((blocks, 4 * part, inner), BF),
    ]


def backward_kernel(
    frames,
    grad_ref,
    stream_ref,
    tokens_ref,
    codes_ref,
    table_ref,
    gain_sp_ref,
    gain_tm_ref,
    gain_ff_out,
    w_qkv_sp_ref,
    w_out_sp_ref,
    w_qkv_tm_ref,
    w_out_tm_ref,
    *refs,
):
    time_saved, space_saved, refs = refs[:3], refs[3:6], refs[6:]
    rest_in, mixed_ref, out_ref, space_total, time_total, rest_total, small_ref, mixed_out_ref, *refs = refs
    small_clips, seen_ref, mixed_sems, own_sem, stage, stage_sems, landing, *refs = refs
    slots, refs = refs[:3], refs[3:]
    time_load_sems, space_load_sems, rest_load_sems, w_sum, shared_sum, *refs = refs
    grad_whole_ref, packed_ref, time_sems, space_sems, *refs = refs
    whole_ref, qkv_ref, att_ref = slots
    blocks, _, part, width = grad_whole_ref.shape
    rows = 4 * part
    group = Group(frames, True)
    group.meet()
    time_gather = Gather(group, grad_whole_ref, time_sems)
    space_gather = Gather(group, grad_whole_ref, space_sems)
    scatter = Scatter(group, *refs[:6])
    rest_load = Move([(rest_in, shared_sum)], rest_load_sems)
    rest_reduce = Reduce(2, 1, rest_load, group, shared_sum, rest_total, *refs[6:9])
    time_reduce = Reduce(2, 1, None, group, w_sum, time_total, *refs[9:12])
    space_reduce = Reduce(1, 0, None, group, shared_sum, space_total, *refs[6:8], refs[12])
    small = SmallSum(group, small_ref, *refs[13:])
    exchange = Exchange(group, stage, landing, stage_sems)
    mixed_bulk = Bulk(group, mixed_ref, mixed_out_ref, mixed_sems, own_sem)
    time_load = Move(list(zip(time_saved, slots)), time_load_sems)
    space_load = Move(list(zip(space_saved, slots)), space_load_sems, blocks)
    ahead = whole_ref.shape[0] - 1

    def gather_grad(gather, block, grad):
        grad_whole_ref[block, group.me] = grad.astype(BF)
        gather.start(block)

    each_block(blocks, lambda block: gather_grad(time_gather, block, grad_ref[block]))
    each_block(ahead, time_load.start)
    each_block(CHUNKS, rest_load.start)
    mixed_bulk.start()
    w_sum[...] = jnp.zeros_like(w_sum)
    seen_ref[...] = visible(rows, frames, 1).astype(F32)
    small_ref[...] = jnp.zeros_like(small_ref)
    small_ref[10:11, :] = gain_ff_out[...]

    def back(block, at, w_qkv_ref):
        scatter.free(at)
        scatter.send(at, sum(dot(packed_ref[block, member], w_qkv_ref[member], (1, 1)) for member in range(3)))

    def attention(block, slot, w_out_ref, sums, seen):
        grad_y = grad_whole_ref[block].reshape(rows, width)
        grad_att = dot(grad_y, w_out_ref[...], (1, 1)).astype(BF)
        grads = attend_back(qkv_ref[slot, 0], qkv_ref[slot, 1], qkv_ref[slot, 2], grad_att, seen)
        for member in range(3):
            packed_ref[block, member] = grads[member]
        piece = sums.shape[1:]
        normed = whole_ref[slot].reshape(rows, width)
        quarter = width // 4
        for member in range(4):
            small = packed_ref[block, member] if member < 3 else att_ref[slot]
            wide = normed if member < 3 else grad_y
            grad_w = dot(small, wide, (0, 0))
            cuts = [grad_w[:, k * quarter : (k + 1) * quarter] for k in range(4)]
            for k in range(2):
                sums[2 * member + k] += jnp.concatenate(cuts[2 * k : 2 * k + 2], axis=0).reshape(piece)

    def time_compute(block):
        time_load.wait(block)

        @pl.when(block + ahead < blocks)
        def _():
            time_load.start(block + ahead)

        @pl.when(block + ahead >= blocks)
        def _():
            space_load.start(block + ahead - blocks)

        attention(block, block % (ahead + 1), w_out_tm_ref, w_sum, seen_ref)
        time_gather.sent(block)
        back(block, block, w_qkv_tm_ref)

    def time_take(block):
        stream = unpack(stream_ref[block], width)
        grad_part, grad_gain = norm_backward(scatter.take(block), stream, row_of(gain_tm_ref))
        exchange.push(block, grad_ref[block] + grad_part)
        small_ref[9:10, :] += grad_gain

    def space_compute(block):
        space_load.wait(block)

        @pl.when(block + ahead < blocks)
        def _():
            space_load.start(block + ahead)

        attention(block, (block + blocks) % (ahead + 1), w_out_sp_ref, shared_sum, None)

    def space_back(pair):
        for k in range(2):
            back(2 * pair + k, 2 * pair + k + blocks, w_qkv_sp_ref)

    def space_take(pair):
        for k in range(2):
            block = 2 * pair + k
            stream = space_stream(tokens_ref, codes_ref, table_ref, block)
            grad_part, grad_gain = norm_backward(scatter.take(block + blocks), stream, row_of(gain_sp_ref))
            grad_stream = unpack(landing[block], width) + grad_part
            out_ref[block] = grad_stream
            small_ref[8:9, :] += grad_gain
            small_clips[pl.ds(block, 1)] = jnp.sum(grad_stream, axis=0, keepdims=True)[None]

    launch_lag = LAG + 2
    space_first = blocks + GAP
    space_done = space_first + blocks
    taken = space_done + blocks // 2 + LAG - 1

    def beside(i):
        block = i - launch_lag

        @pl.when((block >= 0) & (block < blocks))
        def _():
            exchange.arrive(block)
            gather_grad(space_gather, block, unpack(landing[block], width))

        rest_reduce.tick(i)
        time_reduce.tick(i - blocks)

        @pl.when(i == space_first)
        def _():
            shared_sum[...] = jnp.zeros_like(shared_sum)

        @pl.when(i == space_done - 1)
        def _():
            rest_reduce.finish()

        space_reduce.tick(i - space_done)

        @pl.when(i == taken)
        def _():
            for clip in range(blocks):
                small_ref[0:8, :] += coded_rows(codes_ref, clip, 8) * small_clips[clip]

        small.tick(i - taken)

    pipeline(
        [
            (blocks, [time_gather], [(scatter, 0)], time_compute, time_take),
            (GAP, [], [], lambda block: None, None),
            (blocks, [space_gather], [], space_compute, None),
            (blocks // 2, [], [(Twice(scatter, blocks), 0)], space_back, space_take),
        ],
        max(space_done + space_reduce.last() + 1, taken + small.last() + 1),
        beside,
    )
    each_block(blocks, space_gather.sent)
    each_block(blocks, exchange.sent)
    for moved in (time_reduce, space_reduce, small, mixed_bulk):
        moved.finish()


def backward(frames, grad, stream, tokens, codes, table, gains, weights, kept, rest_sum, mixed):
    blocks, part, width = tokens.shape
    inner = weights[1].shape[0]
    rows = 4 * part
    packed = packed_shape(blocks, frames, part, width)
    sums = (CHUNKS, frames, 2 * inner // frames, width // 4)
    small = (16, width)
    peers = 2 + frames.bit_length() - 1
    reduce = Reduce.scratch(sums)
    return call(
        functools.partial(backward_kernel, frames),
        "backward",
        2,
        inside(grad, stream, tokens)
        + scalars(codes)
        + inside(table, *gains, *weights)
        + outside(*kept, rest_sum, mixed),
        inside(jax.ShapeDtypeStruct(tokens.shape, F32))
        + inside(*[jax.ShapeDtypeStruct(sums, BF)] * 3, jax.ShapeDtypeStruct(small, F32))
        + outside(jax.ShapeDtypeStruct(mixed.shape, BF)),
        [pltpu.VMEM((blocks, 1, width), F32), pltpu.VMEM((rows, rows), F32)]
        + Bulk.scratch(frames)
        + Exchange.scratch(packed)
        + [pltpu.VMEM(packed, BF)]
        + [pltpu.VMEM((3,) + each.shape[1:], BF) for each in kept[:3]]
        + [pltpu.SemaphoreType.DMA((3, blocks))] * 2
        + [pltpu.SemaphoreType.DMA((1, CHUNKS)), pltpu.VMEM(sums, F32), pltpu.VMEM(sums, F32)]
        + [pltpu.VMEM((blocks, 4, part, width), BF), pltpu.VMEM((blocks, 3, rows, inner), BF)]
        + [Gather.scratch(blocks)] * 2
        + Scatter.scratch(2 * blocks, blocks, part, width)
        + reduce
        + reduce
        + reduce[2:]
        + SmallSum.scratch(peers, small),
        1 << 30,
    )


def gelu_parts(hidden):
    slope = 0.7978845608028654
    square = hidden * hidden
    bent = jnp.tanh(slope * hidden * (1.0 + 0.044715 * square))
    half = 0.5 * (1.0 + bent)
    grad = half + 0.5 * hidden * (1.0 - bent * bent) * (slope * (1.0 + 3 * 0.044715 * square))
    return hidden * half, grad


def forward_kernel(
    frames,
    tokens_ref,
    codes_ref,
    table_ref,
    cot_in,
    gain_sp_ref,
    gain_tm_ref,
    gain_ff_ref,
    w_qkv_sp_ref,
    w_out_sp_ref,
    w_qkv_tm_ref,
    w_out_tm_ref,
    w_up_in,
    w_down_in,
    stream_ref,
    mixed_ref,
    grad_ref,
    gain_out_ref,
    total_ref,
    sum_out,
    *refs,
):
    space_saved, time_saved, refs = refs[:3], refs[3:6], refs[6:]
    w_sum, rest_sum, sum_sems, w_up_ref, w_down_ref, w_sems, *refs = refs
    whole_ref, qkv_ref, att_ref, space_sems, time_sems, seen_ref, stage, stage_sems, *refs = refs
    cot_ref, bulk_sems, own_sem, cot_whole_ref, sp_sems, tm_sems, ffn_sems, cot_sems, *refs = refs
    blocks, _, part, width = whole_ref.shape
    rows = 4 * part
    half = w_up_ref.shape[2] // 2
    group = Group(frames, True)
    group.meet()
    space_gather = Gather(group, whole_ref, sp_sems)
    time_gather = Gather(group, whole_ref, tm_sems)
    ffn_gather = Gather(group, whole_ref, ffn_sems)
    cot_gather = Gather(group, cot_whole_ref, cot_sems)
    scatter = Scatter(group, *refs[:6])
    grad_scatter = Scatter(group, *refs[6:12])
    reduce = Reduce(2, 1, None, group, w_sum, total_ref, *refs[12:])
    exchange = Exchange(group, stage, stream_ref, stage_sems)
    cot_bulk = Bulk(group, cot_in, cot_ref, bulk_sems, own_sem)
    w_load = Move([(w_up_in, w_up_ref), (w_down_in, w_down_ref)], w_sems)
    sum_save = Move([(rest_sum, sum_out)], sum_sems)

    def gather_normed(gather, block, stream, gain_ref):
        unit, _ = norm_parts(stream)
        whole_ref[block, group.me] = (unit * row_of(gain_ref)).astype(BF)
        gather.start(block)

    def begin(block):
        gather_normed(space_gather, block, space_stream(tokens_ref, codes_ref, table_ref, block), gain_sp_ref)

    each_block(blocks, begin)
    cot_bulk.start()
    w_load.start(0)
    seen_ref[...] = visible(rows, frames).astype(F32)
    w_sum[...] = jnp.zeros_like(w_sum)
    rest_sum[...] = jnp.zeros_like(rest_sum)
    gain_out_ref[...] = jnp.zeros_like(gain_out_ref)

    def attention(block, gather, saved, sems, w_qkv_ref, w_out_ref, seen, at):
        whole_save = Move([(whole_ref, saved[0])], sems.at[0:1])
        save = Move([(qkv_ref, saved[1]), (att_ref, saved[2])], sems.at[1:3])
        whole_save.start(block)

        @pl.when(block >= 2)
        def _():
            save.wait(block - 2)

        slot = block % 2
        result = attention_block(whole_ref.at[block], w_qkv_ref, w_out_ref, qkv_ref.at[slot], att_ref.at[slot], seen)
        save.start(block)
        gather.sent(block)
        whole_save.wait(block)
        scatter.free(at)
        scatter.send(at, result)

        @pl.when(block == blocks - 1)
        def _():
            save.wait(blocks - 2)
            save.wait(blocks - 1)

    def space_compute(block):
        attention(block, space_gather, space_saved, space_sems, w_qkv_sp_ref, w_out_sp_ref, None, block)

    def time_compute(block):
        at = block + blocks
        attention(block, time_gather, time_saved, time_sems, w_qkv_tm_ref, w_out_tm_ref, seen_ref, at)

    def space_take(block):
        exchange.push(block, space_stream(tokens_ref, codes_ref, table_ref, block) + scatter.take(block))

    def time_take(block):
        stream = unpack(stream_ref[block], width) + scatter.take(block + blocks)
        grad_ref[block] = stream
        gather_normed(ffn_gather, block, stream, gain_ff_ref)
        cot_whole_ref[block, group.me] = unpack(cot_ref[:, block], width).astype(BF)
        cot_gather.start(block)

    def ffn_compute(block, second):
        sums = rest_sum if second else w_sum
        hidden = pl.ds(half if second else 0, half)
        normed = whole_ref[block].reshape(rows, width)
        grad_y = cot_whole_ref[block].reshape(rows, width)
        w_up = w_up_ref[0, :, hidden]
        w_down = w_down_ref[0, hidden, :]
        activated, slope = gelu_parts(dot(normed, w_up, (1, 0)))
        activated = activated.astype(BF)
        grad_pre = (dot(grad_y, w_down, (1, 1)) * slope).astype(BF)
        if not second:
            scatter.free(block + 2 * blocks)
        for each, at, values in (
            (scatter, block + 2 * blocks, dot(activated, w_down, (1, 0))),
            (grad_scatter, block, dot(grad_pre, w_up, (1, 1))),
        ):
            if second:
                each.send(at, values, True)
            else:
                each.put(at, values)
        for first, small, wide in ((0, grad_pre, normed), (4, activated, grad_y)):
            grad_w = dot(small, wide, (0, 0))
            for k in range(4):
                cut = grad_w[:, k * (width // 4) : (k + 1) * (width // 4)]
                sums[first + k] += cut.reshape(sums.shape[1:])

    def take(block):
        stream = grad_ref[block]
        for frame, piece in enumerate(pack(stream + scatter.take(block + 2 * blocks), frames)):
            mixed_ref[frame, block] = piece.astype(BF)
        grad_part, grad_gain = norm_backward(grad_scatter.take(block), stream, row_of(gain_ff_ref))
        grad_ref[block] = cot_whole_ref[block, group.me].astype(F32) + grad_part
        gain_out_ref[...] += grad_gain

    launch_lag = LAG + 2
    ffn_first = 2 * blocks + GAP

    def beside(i):
        block = i - launch_lag

        @pl.when((block >= 0) & (block < blocks))
        def _():
            exchange.arrive(block)
            gather_normed(time_gather, block, unpack(stream_ref[block], width), gain_tm_ref)

        @pl.when(i == blocks + GAP)
        def _():
            cot_bulk.finish()

        @pl.when(i == ffn_first)
        def _():
            w_load.wait(0)

        reduce.tick(i - ffn_first - blocks)

        @pl.when(i == ffn_first + 2 * blocks)
        def _():
            each_block(CHUNKS, sum_save.start)

    pipeline(
        [
            (blocks, [space_gather], [(scatter, 0)], space_compute, space_take),
            (GAP, [], [], lambda block: None, None),
            (blocks, [time_gather], [(scatter, blocks)], time_compute, time_take),
            (blocks, [ffn_gather, cot_gather], [], lambda block: ffn_compute(block, False), None),
            (blocks, [], [(scatter, 2 * blocks), (grad_scatter, 0)], lambda block: ffn_compute(block, True), take),
        ],
        ffn_first + blocks + reduce.last() + 1,
        beside,
    )
    each_block(blocks, ffn_gather.sent)
    each_block(blocks, cot_gather.sent)
    each_block(blocks, exchange.sent)
    reduce.finish()
    each_block(CHUNKS, sum_save.wait)


def forward(frames, tokens, codes, table, cot, gains, w_qkv_sp, w_out_sp, w_qkv_tm, w_out_tm, w_up, w_down):
    blocks, part, width = tokens.shape
    inner = w_out_sp.shape[0]
    packed = packed_shape(blocks, frames, part, width)
    whole = pltpu.VMEM((blocks, 4, part, width), BF)
    saved = saved_shapes(blocks, part, width, inner)
    sums = jax.ShapeDtypeStruct((CHUNKS, frames, w_up.shape[1] // (2 * frames), width // 4), F32)
    weights = [w_up[None], w_down[None]]
    return call(
        functools.partial(forward_kernel, frames),
        "forward_and_ffn",
        1,
        inside(tokens)
        + scalars(codes)
        + inside(table)
        + outside(cot)
        + inside(*gains, w_qkv_sp, w_out_sp, w_qkv_tm, w_out_tm)
        + outside(*weights),
        inside(
            jax.ShapeDtypeStruct(packed, BF),
            jax.ShapeDtypeStruct(cot.shape, BF),
            jax.ShapeDtypeStruct((blocks, part, width), F32),
            jax.ShapeDtypeStruct((1, width), F32),
            jax.ShapeDtypeStruct(sums.shape, BF),
        )
        + outside(sums, *saved, *saved),
        [pltpu.VMEM(sums.shape, F32), pltpu.VMEM(sums.shape, F32), pltpu.SemaphoreType.DMA((1, CHUNKS))]
        + held_like(weights)
        + [
            whole,
            pltpu.VMEM((2,) + saved[1].shape[1:], BF),
            pltpu.VMEM((2,) + saved[2].shape[1:], BF),
            pltpu.SemaphoreType.DMA((3, blocks)),
            pltpu.SemaphoreType.DMA((3, blocks)),
            pltpu.VMEM((4 * part, 4 * part), F32),
        ]
        + Exchange.scratch(packed)
        + [pltpu.VMEM(cot.shape, BF)]
        + Bulk.scratch(frames)
        + [whole]
        + [Gather.scratch(blocks)] * 4
        + Scatter.scratch(3 * blocks, blocks, part, width)
        + Scatter.scratch(blocks, blocks, part, width)
        + Reduce.scratch(sums.shape),
        (16 * inner + 12 * w_up.shape[1]) * blocks * 4 * part * width,
    )


def widen_kernel(frames, space_ref, time_ref, first_ref, second_ref, mixed_ref, small_ref, *outs):
    step = pl.program_id(0)
    mixed_out, table_out, *gain_outs = outs[:5]
    for sums_ref, qkv_out, w_out_out in ((space_ref, *outs[5:7]), (time_ref, *outs[7:9])):
        quarter = sums_ref.shape[3]

        @pl.when(step < 3)
        def _():
            for k in range(4):
                qkv_out[0, k * quarter : (k + 1) * quarter] = sums_ref[k // 2, k % 2].astype(F32).T

        @pl.when(step == 3)
        def _():
            for k in range(4):
                w_out_out[:, k * quarter : (k + 1) * quarter] = sums_ref[k // 2, k % 2].astype(F32)

    up_out, down_out = outs[9:]

    @pl.when(step < 2)
    def _():
        for k, ffn_ref in enumerate((first_ref, second_ref)):
            _, hidden, quarter = ffn_ref.shape
            for c in range(2):
                rows, cols = pl.ds(c * quarter, quarter), pl.ds(k * hidden, hidden)
                up_out[rows, cols] = ffn_ref[c].astype(F32).T

    @pl.when(step >= 2)
    def _():
        for k, ffn_ref in enumerate((first_ref, second_ref)):
            _, hidden, quarter = ffn_ref.shape
            for c in range(2):
                rows, cols = pl.ds(k * hidden, hidden), pl.ds(c * quarter, quarter)
                down_out[rows, cols] = ffn_ref[c].astype(F32)

    for block in range(mixed_ref.shape[1]):
        mixed_out[block] = unpack(mixed_ref[:, block], mixed_out.shape[2]).astype(BF)

    @pl.when(step == 0)
    def _():
        table_out[...] = small_ref[0:8, :]
        for k, gain_out in enumerate(gain_outs):
            gain_out[...] = small_ref[8 + k : 9 + k, :]


def widen(frames, space_sums, time_sums, first_sums, second_sums, mixed, small, part, inner):
    width = small.shape[1]
    half = width // 2
    blocks = mixed.shape[1]
    hidden = 2 * first_sums.shape[1] * first_sums.shape[2]
    last_qkv = lambda i: (jnp.minimum(i, 2), 0, 0)
    whole = lambda i: (0, 0)
    turned = [
        (jax.ShapeDtypeStruct((3, width, inner), F32), pl.BlockSpec((1, width, inner), last_qkv)),
        (jax.ShapeDtypeStruct((inner, width), F32), pl.BlockSpec((inner, width), whole)),
    ]
    outs = [
        (jax.ShapeDtypeStruct((blocks, part, width), BF), pl.BlockSpec((blocks // 4, part, width), lambda i: (i, 0, 0))),
        (jax.ShapeDtypeStruct((8, width), F32), pl.BlockSpec((8, width), whole)),
    ]
    outs += [(jax.ShapeDtypeStruct((1, width), F32), pl.BlockSpec((1, width), whole))] * 3 + turned + turned
    outs += [
        (jax.ShapeDtypeStruct((width, hidden), F32), pl.BlockSpec((half, hidden), lambda i: (jnp.minimum(i, 1), 0))),
        (
            jax.ShapeDtypeStruct((hidden, width), F32),
            pl.BlockSpec((hidden, half), lambda i: (0, jnp.maximum(i - 2, 0))),
        ),
    ]
    quarter = width // 4
    chunk = pl.BlockSpec((2, 2, inner, quarter), lambda i: (i, 0, 0, 0))
    ffn_chunk = pl.BlockSpec((2, hidden // 2, quarter), lambda i: (i, 0, 0))
    return pl.pallas_call(
        functools.partial(widen_kernel, frames),
        name="widen",
        grid=(4,),
        out_shape=[shape for shape, _ in outs],
        in_specs=[
            chunk,
            chunk,
            ffn_chunk,
            ffn_chunk,
            pl.BlockSpec((frames, blocks // 4) + mixed.shape[2:], lambda i: (0, i, 0, 0)),
            pl.BlockSpec(small.shape, whole),
        ],
        out_specs=[spec for _, spec in outs],
        compiler_params=pltpu.CompilerParams(vmem_limit_bytes=LIMIT),
    )(
        space_sums.reshape(CHUNKS, 2, inner, quarter),
        time_sums.reshape(CHUNKS, 2, inner, quarter),
        first_sums.reshape(CHUNKS, hidden // 2, quarter),
        second_sums.reshape(CHUNKS, hidden // 2, quarter),
        mixed,
        small,
    )


def pack_rows(values, frames):
    blocks, part, width = values.shape
    shape = packed_shape(blocks, frames, part, width)
    cut = values.reshape(blocks, frames, part // frames, width // shape[-1], shape[-1])
    return cut.transpose(1, 0, 3, 2, 4).reshape((frames, blocks) + shape[2:])


def body(
    frames,
    tokens,
    codes,
    table,
    gain_space,
    gain_time,
    gain_ffn,
    w_qkv_space,
    w_out_space,
    w_qkv_time,
    w_out_time,
    w_up,
    w_down,
    cotangent,
):
    gain_sp, gain_tm, gain_ff = gain_space, gain_time, gain_ffn
    w_qkv_sp = w_qkv_space.swapaxes(0, 1)
    w_qkv_tm = w_qkv_time.swapaxes(0, 1)
    _, blocks, part, width = tokens.shape

    gains = gain_sp, gain_tm, gain_ff
    weights = w_qkv_sp, w_out_space, w_qkv_tm, w_out_time, w_up, w_down
    stream_one, mixed, grad_two, grad_gain_ff, first_totals, ffn_sums, *kept = forward(
        frames, tokens[0], codes, table, pack_rows(cotangent[0], frames), gains, *weights
    )
    grad_zero, space_totals, time_totals, ffn_totals, small, mixed = backward(
        frames,
        grad_two,
        stream_one,
        tokens[0],
        codes,
        table,
        (gain_sp, gain_tm, grad_gain_ff),
        weights[:4],
        kept[3:] + kept[:3],
        ffn_sums,
        mixed,
    )
    mixed, grad_tab, gain_sp, gain_tm, gain_ff, *grads = widen(
        frames, space_totals, time_totals, first_totals, ffn_totals, mixed, small, part, w_out_space.shape[0]
    )
    return (
        mixed[None],
        grad_zero[None],
        grad_tab,
        gain_sp[0],
        gain_tm[0],
        gain_ff[0],
        grads[0].swapaxes(0, 1),
        grads[1],
        grads[2].swapaxes(0, 1),
        grads[3],
        *grads[4:],
    )


def solution(mesh):
    rows = P("frames", None, "tensor", None)
    return jax.shard_map(
        functools.partial(body, mesh.shape["frames"]),
        mesh=mesh,
        in_specs=(
            rows,
            P("frames", None),
            P(),
            P(),
            P(),
            P(),
            P(None, None, "tensor"),
            P("tensor", None),
            P(None, None, "tensor"),
            P("tensor", None),
            P(None, "tensor"),
            P("tensor", None),
            rows,
        ),
        out_specs=(
            rows,
            rows,
            P(),
            P(),
            P(),
            P(),
            P(None, None, "tensor"),
            P("tensor", None),
            P(None, None, "tensor"),
            P("tensor", None),
            P(None, "tensor"),
            P("tensor", None),
        ),
        check_vma=False,
    )
```

time: 1650 us -> 441 us (0.27)
  waiting for transfers between devices: 1270 us -> 0 us
  Pallas kernels: 0 us -> 435 us
  matrix products: 130 us -> 0 us
  other arithmetic: 103 us -> 0 us
  local copies, waits for them, and re-layouts: 74.5 us -> 5.45 us
  blocking collectives: 40.3 us -> 0 us
    reduce_scatter x7 -> x0, waiting for transfers between devices: 604 us -> none  [the longest x1 276 us: body(): lax.psum_scatter(jnp.concatenate([grad_k_part, grad_v_part], axis=-1).ast...]
    pallas_call x0 -> x3, Pallas kernels: none -> 435 us  [the longest x2 424 us: call(): pl.pallas_call(kernel, name=name, out_shape=[shape for shape, _ in outs],...]
    all_gather x8 -> x0, waiting for transfers between devices: 400 us -> none  [the longest x1 121 us: body(): lax.all_gather(keys_tm, 'frames', axis=0, tiled=True)]
    psum x1 -> x0, waiting for transfers between devices: 266 us -> none  [body(): lax.psum(grad_w_qkv_sp.astype(jnp.bfloat16), 'frames').astype(jnp.float32)]
    dot_general x25 -> x0, matrix products: 130 us -> none  [the longest x3 19.7 us: out_backward(): jnp.einsum('fcsd,ed->fcse', grad_y, w_out, preferred_element_type=jnp.flo...]
    psum x1 -> x0, blocking collectives: 40.3 us -> none  [body(): lax.psum((grad_tab, grad_gain_sp, grad_gain_tm, grad_gain_ff), ('tensor',...]
    unnamed x130 -> x1, local copies, waits for them, and re-layouts: 38.7 us -> 3.16 us
    dot_general x4 -> x0, other arithmetic: 31.4 us -> none  [the longest x1 11.9 us: time_probs(): jnp.einsum('fcphe,gcphe->cphfg', split_heads(grad_out), split_heads(value...]
  transfers between devices with their start and end apart: 16 -> 0, of which waited for: 16 -> 0; matrix products, arithmetic and copies ran while one was open for 6% -> 0% of each run, Pallas kernels for 0% -> 0%
where the time goes in v1:
time: 441 us
  Pallas kernels  435 us (99%)
  local copies, waits for them, and re-layouts  5.45 us (1%)
    pallas_call x2, Pallas kernels, call(): pl.pallas_call(kernel, name=name, out_shape=[shape for shape, _ in outs],...  424 us
    pallas_call x1, Pallas kernels, widen(): pl.pallas_call(functools.partial(widen_kernel, frames), name='widen', gri...  10.9 us

profile of v1, /device:TPU:0, one launch (start us, length us, event | category | flops | bytes accessed | tf_op | source)
XLA Modules:
  0.0 440.8 jit_solution(711729825521553475)
XLA Ops:
  0.6 2.3 copy.27
  2.9 215.4 %forward_and_ffn.1 = (bf16[8,8,16,512]{3,2,1,0:T(8,128)(2,1)}, bf16[8,8,16,512]{3,2,1,0:T(8,128)(2,1)}, f32[8,64,1024]{2,1,0:T(8,128)}, f32[1,1024]{1,0:T(1,128)...) custom-call(bf16[8,64,1024]{2,1,0:T(8,128)(2,1)} %bitcast.31, ...), custom_call_target="tpu_custom_call" | custom-call | flops 34359738368 | bytes 16777216 | tf_op jit(solution)/shard_map/forward_and_ffn/pallas_call | solution.py:577
  218.4 208.4 %backward.1 = (f32[8,64,1024]{2,1,0:T(8,128)}, bf16[8,8,64,256]{3,2,1,0:T(8,128)(2,1)}, bf16[8,8,64,256]{3,2,1,0:T(8,128)(2,1)}, bf16[8,8,64,256]{3,2,1,0:T(8,12...) custom-call(f32[8,64,1024]{2,1,0:T(8,128)} %get-tuple-element.41.grad_ref, ...), custom_call_target="tpu_custom_call" | custom-call | flops 1073741824 | bytes 16777216 | tf_op jit(solution)/shard_map/backward/pallas_call | solution.py:577
  426.8 10.9 %widen.1 = (bf16[8,64,1024]{2,1,0:T(8,128)(2,1)}, f32[8,1024]{1,0:T(8,128)}, f32[1,1024]{1,0:T(1,128)}, f32[1,1024]{1,0:T(1,128)}, f32[1,1024]{1,0:T(1,128)}, /*...) custom-call(bf16[8,2,256,256]{3,2,1,0:T(8,128)(2,1)} %bitcast.24, ...), custom_call_target="tpu_custom_call" | custom-call | tf_op jit(solution)/shard_map/widen/pallas_call | solution.py:1126
  437.6 3.2 copy.29

commit v2 on v1

--- a/solution.py
+++ b/solution.py
@@ -308,10 +308,11 @@
 
 
 class Reduce:
-    def __init__(self, group_size, slack, load, group, source, result, stage, landing, sems):
+    def __init__(self, group_size, slack, load, group, source, result, stage, landing, sems, own, own_sems):
         self.group_size, self.slack, self.load = group_size, slack, load
         self.group, self.source, self.result = group, source, result
         self.stage, self.landing, self.sems = stage, landing, sems
+        self.own, self.own_sems = own, own_sems
         self.chunks, self.pieces = result.shape[:2]
         self.levels = group.levels
 
@@ -319,7 +320,7 @@
         return self.pieces >> (level + 1)
 
     def choice(self, chunk, level, normal):
-        turned = 1 - (chunk + self.chunks - 1) // self.chunks
+        turned = self.group.c * (1 - (chunk + self.chunks - 3) // self.chunks)
         return normal[level] + turned * (normal[(level + 1) % self.levels] - normal[level])
 
     def bit(self, chunk, level):
@@ -348,7 +349,12 @@
 
     def up(self, chunk, level):
         done = self.result.at[chunk, pl.ds(self.offset(chunk, level + 1), self.half(level))]
-        return remote(done, done, self.sems, self.levels + level, chunk, self.partner(chunk, level), "frames")
+        source = self.own.at[chunk] if level == self.levels - 1 else done
+        return remote(source, done, self.sems, self.levels + level, chunk, self.partner(chunk, level), "frames")
+
+    def keep(self, chunk):
+        mine = self.result.at[chunk, pl.ds(self.offset(chunk, self.levels), 1)]
+        return pltpu.make_async_copy(self.own.at[chunk], mine, self.own_sems.at[chunk])
 
     def put(self, chunk, level):
         half = self.half(level)
@@ -373,9 +379,12 @@
         elif turn == levels:
             self.add(chunk, levels - 1)
             mine = pl.ds(self.offset(chunk, levels), 1)
-            self.result[chunk, mine] = self.source[chunk, mine].astype(BF)
+            self.own[chunk] = self.source[chunk, mine].astype(BF)
+            self.keep(chunk).start()
             self.up(chunk, levels - 1).start()
         else:
+            if turn == levels + 1:
+                self.keep(chunk).wait()
             self.up(chunk, 2 * levels - turn).wait_recv()
             self.up(chunk, 2 * levels - turn - 1).start()
 
@@ -393,6 +402,8 @@
 
     def finish(self):
         def done(chunk, carry):
+            if self.levels == 1:
+                self.keep(chunk).wait()
             self.up(chunk, 0).wait_recv()
             for level in range(self.levels):
                 self.down(chunk, level).wait_send()
@@ -409,6 +420,8 @@
             pltpu.VMEM((chunks, pieces - 1, part, width), BF),
             pltpu.VMEM((chunks, pieces - 1, part, width), BF),
             pltpu.SemaphoreType.DMA((2, 2 * levels, chunks)),
+            pltpu.VMEM((chunks, 1, part, width), BF),
+            pltpu.SemaphoreType.DMA((chunks,)),
         ]
 
 
@@ -645,10 +658,10 @@
     space_gather = Gather(group, grad_whole_ref, space_sems)
     scatter = Scatter(group, *refs[:6])
     rest_load = Move([(rest_in, shared_sum)], rest_load_sems)
-    rest_reduce = Reduce(2, 1, rest_load, group, shared_sum, rest_total, *refs[6:9])
-    time_reduce = Reduce(2, 1, None, group, w_sum, time_total, *refs[9:12])
-    space_reduce = Reduce(1, 0, None, group, shared_sum, space_total, *refs[6:8], refs[12])
-    small = SmallSum(group, small_ref, *refs[13:])
+    rest_reduce = Reduce(2, 1, rest_load, group, shared_sum, rest_total, *refs[6:11])
+    time_reduce = Reduce(2, 1, None, group, w_sum, time_total, *refs[11:16])
+    space_reduce = Reduce(1, 0, None, group, shared_sum, space_total, *refs[6:8], *refs[16:19])
+    small = SmallSum(group, small_ref, *refs[19:])
     exchange = Exchange(group, stage, landing, stage_sems)
     mixed_bulk = Bulk(group, mixed_ref, mixed_out_ref, mixed_sems, own_sem)
     time_load = Move(list(zip(time_saved, slots)), time_load_sems)
@@ -800,7 +813,8 @@
         + inside(table, *gains, *weights)
         + outside(*kept, rest_sum, mixed),
         inside(jax.ShapeDtypeStruct(tokens.shape, F32))
-        + inside(*[jax.ShapeDtypeStruct(sums, BF)] * 3, jax.ShapeDtypeStruct(small, F32))
+        + outside(*[jax.ShapeDtypeStruct(sums, BF)] * 3)
+        + inside(jax.ShapeDtypeStruct(small, F32))
         + outside(jax.ShapeDtypeStruct(mixed.shape, BF)),
         [pltpu.VMEM((blocks, 1, width), F32), pltpu.VMEM((rows, rows), F32)]
         + Bulk.scratch(frames)
@@ -1028,9 +1042,8 @@
             jax.ShapeDtypeStruct(cot.shape, BF),
             jax.ShapeDtypeStruct((blocks, part, width), F32),
             jax.ShapeDtypeStruct((1, width), F32),
-            jax.ShapeDtypeStruct(sums.shape, BF),
         )
-        + outside(sums, *saved, *saved),
+        + outside(jax.ShapeDtypeStruct(sums.shape, BF), sums, *saved, *saved),
         [pltpu.VMEM(sums.shape, F32), pltpu.VMEM(sums.shape, F32), pltpu.SemaphoreType.DMA((1, CHUNKS))]
         + held_like(weights)
         + [
@@ -1053,42 +1066,38 @@
     )
 
 
-def widen_kernel(frames, space_ref, time_ref, first_ref, second_ref, mixed_ref, small_ref, *outs):
+def widen_kernel(space_ref, time_ref, first_ref, second_ref, mixed_ref, tokens_ref, small_ref, *outs):
     step = pl.program_id(0)
-    mixed_out, table_out, *gain_outs = outs[:5]
-    for sums_ref, qkv_out, w_out_out in ((space_ref, *outs[5:7]), (time_ref, *outs[7:9])):
+    mixed_out, tokens_out, table_out, *gain_outs = outs[:6]
+    for sums_ref, qkv_out, w_out_out in ((space_ref, *outs[6:8]), (time_ref, *outs[8:10])):
         quarter = sums_ref.shape[3]
 
-        @pl.when(step < 3)
-        def _():
-            for k in range(4):
-                qkv_out[0, k * quarter : (k + 1) * quarter] = sums_ref[k // 2, k % 2].astype(F32).T
-
-        @pl.when(step == 3)
-        def _():
-            for k in range(4):
-                w_out_out[:, k * quarter : (k + 1) * quarter] = sums_ref[k // 2, k % 2].astype(F32)
-
-    up_out, down_out = outs[9:]
-
-    @pl.when(step < 2)
+        @pl.when(step < 6)
+        def _():
+            for k in range(2):
+                qkv_out[0, k * quarter : (k + 1) * quarter] = sums_ref[0, k].T.astype(F32)
+
+        @pl.when(step >= 6)
+        def _():
+            for k in range(2):
+                w_out_out[:, k * quarter : (k + 1) * quarter] = sums_ref[0, k].astype(F32)
+
+    up_out, down_out = outs[10:]
+    hidden = first_ref.shape[1]
+
+    @pl.when(step < 4)
     def _():
         for k, ffn_ref in enumerate((first_ref, second_ref)):
-            _, hidden, quarter = ffn_ref.shape
-            for c in range(2):
-                rows, cols = pl.ds(c * quarter, quarter), pl.ds(k * hidden, hidden)
-                up_out[rows, cols] = ffn_ref[c].astype(F32).T
-
-    @pl.when(step >= 2)
+            up_out[:, k * hidden : (k + 1) * hidden] = ffn_ref[0].T.astype(F32)
+
+    @pl.when(step >= 4)
     def _():
         for k, ffn_ref in enumerate((first_ref, second_ref)):
-            _, hidden, quarter = ffn_ref.shape
-            for c in range(2):
-                rows, cols = pl.ds(k * hidden, hidden), pl.ds(c * quarter, quarter)
-                down_out[rows, cols] = ffn_ref[c].astype(F32)
+            down_out[k * hidden : (k + 1) * hidden] = ffn_ref[0].astype(F32)
 
     for block in range(mixed_ref.shape[1]):
         mixed_out[block] = unpack(mixed_ref[:, block], mixed_out.shape[2]).astype(BF)
+    tokens_out[...] = tokens_ref[...]
 
     @pl.when(step == 0)
     def _():
@@ -1097,43 +1106,49 @@
             gain_out[...] = small_ref[8 + k : 9 + k, :]
 
 
-def widen(frames, space_sums, time_sums, first_sums, second_sums, mixed, small, part, inner):
-    width = small.shape[1]
-    half = width // 2
-    blocks = mixed.shape[1]
+def widen(frames, space_sums, time_sums, first_sums, second_sums, mixed, tokens, small, inner):
+    blocks, part, width = tokens.shape
+    quarter = width // 4
     hidden = 2 * first_sums.shape[1] * first_sums.shape[2]
-    last_qkv = lambda i: (jnp.minimum(i, 2), 0, 0)
     whole = lambda i: (0, 0)
+    some = pl.BlockSpec((blocks // CHUNKS, part, width), lambda i: (i, 0, 0))
     turned = [
-        (jax.ShapeDtypeStruct((3, width, inner), F32), pl.BlockSpec((1, width, inner), last_qkv)),
-        (jax.ShapeDtypeStruct((inner, width), F32), pl.BlockSpec((inner, width), whole)),
+        (
+            jax.ShapeDtypeStruct((3, width, inner), F32),
+            pl.BlockSpec((1, 2 * quarter, inner), lambda i: (jnp.minimum(i, 5) // 2, jnp.minimum(i, 5) % 2, 0)),
+        ),
+        (
+            jax.ShapeDtypeStruct((inner, width), F32),
+            pl.BlockSpec((inner, 2 * quarter), lambda i: (0, jnp.maximum(i - 6, 0))),
+        ),
     ]
-    outs = [
-        (jax.ShapeDtypeStruct((blocks, part, width), BF), pl.BlockSpec((blocks // 4, part, width), lambda i: (i, 0, 0))),
-        (jax.ShapeDtypeStruct((8, width), F32), pl.BlockSpec((8, width), whole)),
-    ]
+    outs = [(jax.ShapeDtypeStruct(tokens.shape, BF), some), (jax.ShapeDtypeStruct(tokens.shape, F32), some)]
+    outs += [(jax.ShapeDtypeStruct((8, width), F32), pl.BlockSpec((8, width), whole))]
     outs += [(jax.ShapeDtypeStruct((1, width), F32), pl.BlockSpec((1, width), whole))] * 3 + turned + turned
     outs += [
-        (jax.ShapeDtypeStruct((width, hidden), F32), pl.BlockSpec((half, hidden), lambda i: (jnp.minimum(i, 1), 0))),
+        (
+            jax.ShapeDtypeStruct((width, hidden), F32),
+            pl.BlockSpec((quarter, hidden), lambda i: (jnp.minimum(i, 3), 0)),
+        ),
         (
             jax.ShapeDtypeStruct((hidden, width), F32),
-            pl.BlockSpec((hidden, half), lambda i: (0, jnp.maximum(i - 2, 0))),
+            pl.BlockSpec((hidden, quarter), lambda i: (0, jnp.maximum(i - 4, 0))),
         ),
     ]
-    quarter = width // 4
-    chunk = pl.BlockSpec((2, 2, inner, quarter), lambda i: (i, 0, 0, 0))
-    ffn_chunk = pl.BlockSpec((2, hidden // 2, quarter), lambda i: (i, 0, 0))
+    chunk = pl.BlockSpec((1, 2, inner, quarter), lambda i: (i, 0, 0, 0))
+    ffn_chunk = pl.BlockSpec((1, hidden // 2, quarter), lambda i: (i, 0, 0))
     return pl.pallas_call(
-        functools.partial(widen_kernel, frames),
+        widen_kernel,
         name="widen",
-        grid=(4,),
+        grid=(CHUNKS,),
         out_shape=[shape for shape, _ in outs],
         in_specs=[
             chunk,
             chunk,
             ffn_chunk,
             ffn_chunk,
-            pl.BlockSpec((frames, blocks // 4) + mixed.shape[2:], lambda i: (0, i, 0, 0)),
+            pl.BlockSpec((frames, blocks // CHUNKS) + mixed.shape[2:], lambda i: (0, i, 0, 0)),
+            some,
             pl.BlockSpec(small.shape, whole),
         ],
         out_specs=[spec for _, spec in outs],
@@ -1144,6 +1159,7 @@
         first_sums.reshape(CHUNKS, hidden // 2, quarter),
         second_sums.reshape(CHUNKS, hidden // 2, quarter),
         mixed,
+        tokens,
         small,
     )
 
@@ -1194,8 +1210,8 @@
         ffn_sums,
         mixed,
     )
-    mixed, grad_tab, gain_sp, gain_tm, gain_ff, *grads = widen(
-        frames, space_totals, time_totals, first_totals, ffn_totals, mixed, small, part, w_out_space.shape[0]
+    mixed, grad_zero, grad_tab, gain_sp, gain_tm, gain_ff, *grads = widen(
+        frames, space_totals, time_totals, first_totals, ffn_totals, mixed, grad_zero, small, w_out_space.shape[0]
     )
     return (
         mixed[None],

time: 441 us -> 435 us (0.986)
    pallas_call x2, Pallas kernels: 424 us -> 418 us  [call(): pl.pallas_call(kernel, name=name, out_shape=[shape for shape, _ in outs],...]
where the time goes in v2:
time: 435 us; the launch traced here: 434 us
  Pallas kernels  431 us (99%)
    pallas_call x2, Pallas kernels, call(): pl.pallas_call(kernel, name=name, out_shape=[shape for shape, _ in outs],...  418 us
    pallas_call x1, Pallas kernels, widen(): pl.pallas_call(widen_kernel, name='widen', grid=(CHUNKS,), out_shape=[sha...  13.4 us

profile of v2, /device:TPU:0, one launch (start us, length us, event | category | flops | bytes accessed | tf_op | source)
XLA Modules:
  0.0 434.1 jit_solution(7140592396224380419)
XLA Ops:
  0.6 2.3 copy.27
  2.9 213.2 %forward_and_ffn.1 = (bf16[8,8,16,512]{3,2,1,0:T(8,128)(2,1)}, bf16[8,8,16,512]{3,2,1,0:T(8,128)(2,1)}, f32[8,64,1024]{2,1,0:T(8,128)}, f32[1,1024]{1,0:T(1,128)...) custom-call(bf16[8,64,1024]{2,1,0:T(8,128)(2,1)} %bitcast.30, ...), custom_call_target="tpu_custom_call" | custom-call | flops 34359738368 | bytes 16777216 | tf_op jit(solution)/shard_map/forward_and_ffn/pallas_call | solution.py:590
  216.2 204.4 %backward.1 = (f32[8,64,1024]{2,1,0:T(8,128)}, bf16[8,8,64,256]{3,2,1,0:T(8,128)(2,1)}, bf16[8,8,64,256]{3,2,1,0:T(8,128)(2,1)}, bf16[8,8,64,256]{3,2,1,0:T(8,12...) custom-call(f32[8,64,1024]{2,1,0:T(8,128)} %get-tuple-element.42.grad_ref, ...), custom_call_target="tpu_custom_call" | custom-call | flops 1073741824 | bytes 16777216 | tf_op jit(solution)/shard_map/backward/pallas_call | solution.py:590
  420.6 13.4 %widen.1 = (bf16[8,64,1024]{2,1,0:T(8,128)(2,1)}, f32[8,64,1024]{2,1,0:T(8,128)}, f32[8,1024]{1,0:T(8,128)}, f32[1,1024]{1,0:T(1,128)}, f32[1,1024]{1,0:T(1,128)...) custom-call(bf16[8,2,256,256]{3,2,1,0:T(8,128)(2,1)} %bitcast.23, ...), custom_call_target="tpu_custom_call" | custom-call | tf_op jit(solution)/shard_map/widen/pallas_call | solution.py:1140

commit v3 on v2

--- a/solution.py
+++ b/solution.py
@@ -13,8 +13,8 @@
 F32 = jnp.float32
 MESH = pl.DeviceIdType.MESH
 LIMIT = 63 * 1024 * 1024
-LAG = 5
-GAP = 2
+LAG = 4
+GAP = 1
 CHUNKS = 8
 
 

time: 435 us -> 434 us (level)
  no operation moved by 1% of the time
where the time goes in v3:
time: 434 us
  Pallas kernels  431 us (99%)
    pallas_call x2, Pallas kernels, call(): pl.pallas_call(kernel, name=name, out_shape=[shape for shape, _ in outs],...  417 us
    pallas_call x1, Pallas kernels, widen(): pl.pallas_call(widen_kernel, name='widen', grid=(CHUNKS,), out_shape=[sha...  13.4 us

profile of v3, /device:TPU:0, one launch (start us, length us, event | category | flops | bytes accessed | tf_op | source)
XLA Modules:
  0.0 433.9 jit_solution(13871478442628431370)
XLA Ops:
  0.6 2.3 copy.27
  2.9 213.2 %forward_and_ffn.1 = (bf16[8,8,16,512]{3,2,1,0:T(8,128)(2,1)}, bf16[8,8,16,512]{3,2,1,0:T(8,128)(2,1)}, f32[8,64,1024]{2,1,0:T(8,128)}, f32[1,1024]{1,0:T(1,128)...) custom-call(bf16[8,64,1024]{2,1,0:T(8,128)(2,1)} %bitcast.30, ...), custom_call_target="tpu_custom_call" | custom-call | flops 34359738368 | bytes 16777216 | tf_op jit(solution)/shard_map/forward_and_ffn/pallas_call | solution.py:590
  216.2 204.1 %backward.1 = (f32[8,64,1024]{2,1,0:T(8,128)}, bf16[8,8,64,256]{3,2,1,0:T(8,128)(2,1)}, bf16[8,8,64,256]{3,2,1,0:T(8,128)(2,1)}, bf16[8,8,64,256]{3,2,1,0:T(8,12...) custom-call(f32[8,64,1024]{2,1,0:T(8,128)} %get-tuple-element.42.grad_ref, ...), custom_call_target="tpu_custom_call" | custom-call | flops 1073741824 | bytes 16777216 | tf_op jit(solution)/shard_map/backward/pallas_call | solution.py:590
  420.3 13.4 %widen.1 = (bf16[8,64,1024]{2,1,0:T(8,128)(2,1)}, f32[8,64,1024]{2,1,0:T(8,128)}, f32[8,1024]{1,0:T(8,128)}, f32[1,1024]{1,0:T(1,128)}, f32[1,1024]{1,0:T(1,128)...) custom-call(bf16[8,2,256,256]{3,2,1,0:T(8,128)(2,1)} %bitcast.23, ...), custom_call_target="tpu_custom_call" | custom-call | tf_op jit(solution)/shard_map/widen/pallas_call | solution.py:1140
